TPU v7x, 256 devices: a whole 4x4x8 slice. The times are simulated.
256 devices in a mesh: arch: 2 (over core), dom: 128 (over z, y, x).
Axes of the slice: x: 4, y: 4, z: 8, core: 2. Of those that a mesh axis runs over, the one named last changes fastest.
Arguments:
- position: float32 [3, 8388608], P(None, ('arch', 'dom')), may hold values from -6 to 6
- particle_mass: float32 [8388608], P(('arch', 'dom')), may hold values from 0.5 to 2
- settling: float32 [8388608], P(('arch', 'dom')), may hold values from 0.05 to 1
- walk_noise: float32 [3, 3, 8388608], P(None, None, ('arch', 'dom')), may hold values from -6 to 6
- velocity: bfloat16 [4, 3, 256, 2048], P(None, None, ('arch', 'dom')), may hold values from -6 to 6
- diffusivity: bfloat16 [4, 256, 2048], P(None, ('arch', 'dom')), may hold values from 0.019897461 to 0.5
- block_tile: int32 [3, 256, 128], P(None, ('arch', 'dom')), may hold values from 0 to 255, as said below
- cell_index: int32 [3, 8388608], P(None, ('arch', 'dom')), may hold values from 0 to 2047
- bed_cell: int32 [3, 8388608], P(None, ('arch', 'dom')), may hold values from 0 to 511
- route_code: int32 [2, 256, 128], P(None, ('arch', 'dom')), may hold values from 0 to 127, each once within a row
Outputs:
- final_position: float32 [3, 8388608], P(None, ('arch', 'dom'))
- final_mass: float32 [8388608], P(('arch', 'dom'))
- bed_deposit: float32 [256, 512], P(('arch', 'dom'))
Inputs may be any that keep to these rules, and one draw needn't show every extreme that they name: `block_tile`: in every step each block's tile belongs to the group of the block's dom index d: (tile) % 128 equals d. Within each group, tiles held at lower arch indices are used by more blocks than those at higher ones.
All inputs are finite; a program needn't handle non-finite values.
Results may differ from a plain program's by a relative error of at most 0.0003.
Values may be sent and summed in bfloat16 or wider, within the bound.
No kernel may reach another device: no remote copies, remote signals or barrier semaphores. Data moves between devices by JAX's collectives and lax.ppermute only.
A program may use at most 64 MiB of HBM per device.

v0:
```python
import math

import jax
import jax.numpy as jnp
from jax import lax
from jax.sharding import PartitionSpec as P

TILE_ARCH = 1
BEDC = 512


time_step = 0.5


def build_lookup(earlier, later):
    stacked = jnp.concatenate([earlier[0], later[0], earlier[1][None], later[1][None]], 0)
    tile_count = stacked.shape[1]
    return stacked.reshape(8, tile_count, stacked.shape[2] // 128, 128).transpose(1, 0, 2, 3)


def interpolate(lookup, local_tile, cells):
    nblocks = local_tile.shape[0]
    bundle = math.gcd(nblocks, 4)
    tile_count = lookup.shape[0]
    row_count = lookup.shape[2]
    lane_ids = jnp.arange(128, dtype=jnp.int32)
    row_ids = jnp.arange(row_count, dtype=jnp.int32)
    tile_ids = jnp.arange(tile_count, dtype=jnp.int32)

    def interpolate_one_bundle(pieces):
        tile_bundle, cell_bundle = pieces
        column_hit = ((cell_bundle % 128)[..., None] == lane_ids).astype(jnp.bfloat16)
        partial_value = jnp.einsum(
            "tqrc,gpc->gtqrp", lookup, column_hit, preferred_element_type=jnp.float32
        )
        row_hit = ((cell_bundle // 128)[:, None, :] == row_ids[None, :, None]).astype(jnp.float32)
        tile_hit = (tile_bundle[:, None] == tile_ids[None, :]).astype(jnp.float32)
        joint = tile_hit[:, :, None, None] * row_hit[:, None]
        return jnp.sum(partial_value * joint[:, :, None], axis=(1, 3))

    sampled = lax.map(
        interpolate_one_bundle,
        (
            local_tile.reshape(nblocks // bundle, bundle),
            cells.reshape(nblocks // bundle, bundle, -1),
        ),
    )
    return sampled.reshape(nblocks, 8, -1)


def deposit_bed(deposit, local_tile, bed_cells, tile_count):
    nblocks = local_tile.shape[0]
    bundle = math.gcd(nblocks, 8)
    tile_ids = jnp.arange(tile_count, dtype=jnp.int32)
    bed_ids = jnp.arange(BEDC, dtype=jnp.int32)

    def deposit_one_bundle(pieces):
        dep_bundle, tile_bundle, bed_bundle = pieces
        tile_hit = (tile_bundle[:, None] == tile_ids[None, :]).astype(jnp.float32)
        weighted = dep_bundle[:, None, :] * tile_hit[:, :, None]
        bed_hit = (bed_bundle[..., None] == bed_ids).astype(jnp.float32)
        return jnp.einsum("gtw,gwc->tc", weighted, bed_hit, precision=lax.Precision.HIGHEST)

    width = deposit.shape[1]
    pieces = (
        deposit.reshape(nblocks // bundle, bundle, width),
        local_tile.reshape(nblocks // bundle, bundle),
        bed_cells.reshape(nblocks // bundle, bundle, width),
    )
    return jnp.sum(lax.map(deposit_one_bundle, pieces), axis=0)


def permute_blocks(order, state):
    nblocks = order.shape[0]
    slot_ids = jnp.arange(nblocks, dtype=jnp.int32)
    mover = (order[None, :] == slot_ids[:, None]).astype(jnp.float32)
    flat = state.reshape(nblocks, -1)
    moved = jnp.dot(
        mover, flat, precision=lax.Precision.HIGHEST, preferred_element_type=jnp.float32
    )
    return moved.reshape(state.shape)


def body(
    position,
    particle_mass,
    settling,
    walk_noise,
    velocity,
    diffusivity,
    block_tile,
    cell_index,
    bed_cell,
    route_code,
):
    dom_count = lax.axis_size("dom")
    arch_count = lax.axis_size("arch")
    particles = position.shape[1]
    nblocks = block_tile.shape[2]
    width = particles // nblocks
    per_peer = nblocks // dom_count
    tiles_group = TILE_ARCH * arch_count
    slabs = velocity.shape[0]
    steps = cell_index.shape[0]
    places = position.reshape(3, nblocks, width).transpose(1, 0, 2)
    carried = jnp.stack([particle_mass, settling], 0).reshape(2, nblocks, width).transpose(1, 0, 2)
    whole_velocity, whole_diffusivity = (
        lax.all_gather(velocity, "arch", axis=2, tiled=True),
        lax.all_gather(diffusivity, "arch", axis=1, tiled=True),
    )
    archive = [(whole_velocity[slab], whole_diffusivity[slab]) for slab in range(slabs)]
    bed_share = jnp.zeros((TILE_ARCH, BEDC), jnp.float32)
    for step in range(steps):
        lookup = build_lookup(archive[step], archive[step + 1])
        global_tile = block_tile[step, 0]
        local_tile = global_tile // TILE_ARCH // dom_count * TILE_ARCH + global_tile % TILE_ARCH
        cells = cell_index[step].reshape(nblocks, width)
        sampled = interpolate(lookup, local_tile, cells)
        masses = carried[:, 0]
        speeds = carried[:, 1]
        drift = 0.5 * time_step * (sampled[:, 0:3] + sampled[:, 3:6])
        drift = drift.at[:, 2].add(-time_step * speeds)
        noise_now = walk_noise[step].reshape(3, nblocks, width).transpose(1, 0, 2)
        spread = jnp.sqrt(time_step * (sampled[:, 6] + sampled[:, 7]))
        places = places + drift + spread[:, None] * noise_now
        deposit = masses * (1.0 - jnp.exp(-time_step * speeds))
        masses = masses - deposit
        partial_value = deposit_bed(
            deposit, local_tile, bed_cell[step].reshape(nblocks, width), tiles_group
        )
        bed_share = bed_share + lax.psum_scatter(
            partial_value, "arch", scatter_dimension=0, tiled=True
        )
        carried = jnp.stack([masses, speeds], 1)
        if step + 1 < steps:
            order = route_code[step, 0]
            particle_state = jnp.concatenate([places, carried], 1)
            outgoing = permute_blocks(order, particle_state)
            incoming = lax.all_to_all(
                outgoing.reshape(dom_count, per_peer, 5, width),
                "dom",
                split_axis=0,
                concat_axis=0,
                tiled=True,
            )
            incoming = incoming.reshape(nblocks, 5, width)
            places = incoming[:, 0:3]
            carried = incoming[:, 3:5]
    final_places = places.transpose(1, 0, 2).reshape(3, particles)
    final_carried = carried.transpose(1, 0, 2).reshape(2, particles)
    scale_factor = TILE_ARCH * BEDC / particles
    return (final_places, final_carried[0], bed_share * scale_factor)


def solution(mesh):
    return jax.shard_map(
        body,
        mesh=mesh,
        in_specs=(
            P(None, ("arch", "dom")),
            P(("arch", "dom")),
            P(("arch", "dom")),
            P(None, None, ("arch", "dom")),
            P(None, None, ("arch", "dom"), None),
            P(None, ("arch", "dom"), None),
            P(None, ("arch", "dom"), None),
            P(None, ("arch", "dom")),
            P(None, ("arch", "dom")),
            P(None, ("arch", "dom"), None),
        ),
        out_specs=(P(None, ("arch", "dom")), P(("arch", "dom")), P(("arch", "dom"), None)),
        check_vma=False,
    )
```

profile of v0, /device:TPU:1, one launch (start us, length us, event | category | flops | bytes accessed | tf_op | source)
XLA Modules:
  0.0 332.7 jit_solution(807415934628013040)
XLA Ops:
  0.7 1.9 slice_reduce_fusion.11
  2.7 4.9 %all_gather.7 = bf16[4,2,2048]{2,0,1:T(4,128)(2,1)S(1)} all-gather(bf16[4,1,2048]{2,0,1:T(4,128)(2,1)} %param.33), channel_id=1, replica_groups=mesh['arch'=2,'dom'=128] {'arch'}, dimensions={1}, use_global_device_ids=true | all-gather | bytes 49152 | tf_op jit(solution)/shard_map/all_gather | solution.py:109
  7.7 2.2 all_gather.6
  11.3 2.0 slice_reduce_fusion.1
  13.5 21.8 %while.75 = (s32[]{:T(128)}, f32[32,4,8,256]{3,2,1,0:T(8,128)S(1)}, s32[32,4,256]{2,1,0:T(4,128)S(1)}, bf16[2,8,16,128]{3,2,1,0:T(8,128)(2,1)S(1)}, s32[32,4]{1,0:T(8,128)S(1)}, /*index=5*/s32[]{:T(128)}) while((s32[]{:T(128)}, f32[32,4,8,256]{3,2,1,0:T(8,128)S(1)}, s32[32,4,256]{2,1,0:T(4,128)S(1)}, ...), condition=%wide.region_2.3_spmd.clone, body=%wide.region_0.2_spmd.clone.sunk | while | flops 67841040 | bytes 577737 | solution.py:41
  36.4 2.4 fusion.133
  40.8 1.5 copy.70
  42.3 14.0 %all-to-all-start = ((f32[128,1,5,256]{3,1,2,0:T(1,128)}), f32[128,1,5,256]{3,1,2,0:T(1,128)S(1)}, u32[]{:S(2)}, u32[]{:S(2)}) async-start(f32[128,1,5,256]{3,1,2,0:T(1,128)} %copy.70), calls=%async_computation | async-start | bytes 1310720 | tf_op jit(solution)/shard_map/all_to_all | solution.py:139
  58.9 21.8 %while.76 = (s32[]{:T(128)}, f32[32,4,8,256]{3,2,1,0:T(8,128)S(1)}, s32[32,4,256]{2,1,0:T(4,128)S(1)}, bf16[2,8,16,128]{3,2,1,0:T(8,128)(2,1)S(1)}, s32[32,4]{1,0:T(8,128)S(1)}, /*index=5*/s32[]{:T(128)}) while((s32[]{:T(128)}, f32[32,4,8,256]{3,2,1,0:T(8,128)S(1)}, s32[32,4,256]{2,1,0:T(4,128)S(1)}, ...), condition=%wide.region_5.6_spmd.clone, body=%wide.region_3.5_spmd.clone.sunk | while | flops 67841040 | bytes 577737 | solution.py:41
  82.5 33.8 %while.78 = (s32[]{:T(128)}, f32[16,2,512]{2,1,0:T(2,128)}, f32[16,8,256]{2,1,0:T(8,128)S(1)}, s32[16,8]{1,0:T(8,128)S(1)}, s32[16,8,256]{2,1,0:T(8,128)S(1)}, /*index=5*/s32[]{:T(128)}) while((s32[]{:T(128)}, f32[16,2,512]{2,1,0:T(2,128)}, f32[16,8,256]{2,1,0:T(8,128)S(1)}, s32[16,8]{1,0:T(8,128)S(1)}, ...), condition=%wide.region_10.11_spmd.clone, body=%wide.region_9.10_spmd.clone.sunk | while | flops 26218528 | bytes 53565 | solution.py:70
  82.6 2.0 fusion.192
  84.7 2.0 fusion.192
  86.8 2.0 fusion.192
  88.9 2.0 fusion.192
  91.1 2.0 fusion.192
  93.2 2.0 fusion.192
  95.3 2.0 fusion.192
  97.4 2.0 fusion.192
  99.5 2.0 fusion.192
  101.6 2.0 fusion.192
  103.7 2.0 fusion.192
  105.9 2.0 fusion.192
  108.0 2.0 fusion.192
  110.1 2.0 fusion.192
  112.2 2.0 fusion.192
  114.3 2.0 fusion.192
  116.5 91.7 %while.77 = (s32[]{:T(128)}, f32[32,4,8,256]{3,2,1,0:T(8,128)S(1)}, s32[32,4,256]{2,1,0:T(4,128)}, bf16[2,8,16,128]{3,2,1,0:T(8,128)(2,1)}, s32[32,4]{1,0:T(8,128)}, /*index=5*/s32[]{:T(128)}) while((s32[]{:T(128)}, f32[32,4,8,256]{3,2,1,0:T(8,128)S(1)}, s32[32,4,256]{2,1,0:T(4,128)}, bf16[2,8,16,128]{3,2,1,0:T(8,128)(2,1)}, ...), condition=%wide.region_8.9_spmd.clone, body=%wide.region_6.8_spmd.clone.sunk | while | flops 67841040 | bytes 577737 | solution.py:41
  218.4 1.5 copy.77
  219.9 13.0 %all-to-all-start.1 = ((f32[128,1,5,256]{3,1,2,0:T(1,128)}), f32[128,1,5,256]{3,1,2,0:T(1,128)S(1)}, u32[]{:S(2)}, u32[]{:S(2)}) async-start(f32[128,1,5,256]{3,1,2,0:T(1,128)} %copy.77), calls=%async_computation.1 | async-start | bytes 1310720 | tf_op jit(solution)/shard_map/all_to_all | solution.py:139
  233.0 46.4 %while.79 = (s32[]{:T(128)}, f32[16,2,512]{2,1,0:T(2,128)S(1)}, f32[16,8,256]{2,1,0:T(8,128)S(1)}, s32[16,8]{1,0:T(8,128)}, s32[16,8,256]{2,1,0:T(8,128)}, /*index=5*/s32[]{:T(128)}) while((s32[]{:T(128)}, f32[16,2,512]{2,1,0:T(2,128)S(1)}, f32[16,8,256]{2,1,0:T(8,128)S(1)}, s32[16,8]{1,0:T(8,128)}, s32[16,8,256]{2,1,0:T(8,128)}, ...), condition=%wide.region_14.15_spmd.clone, body=%wide.region_13.14_spmd.clone.sunk | while | flops 26218528 | bytes 57597 | solution.py:70
  237.3 1.4 fusion.196
  246.0 1.4 fusion.196
  254.7 1.4 fusion.196
  257.6 1.4 fusion.196
  260.5 1.4 fusion.196
  263.4 1.4 fusion.196
  266.3 1.4 fusion.196
  269.2 1.4 fusion.196
  272.1 1.4 fusion.196
  275.0 1.4 fusion.196
  277.9 1.4 fusion.196
  279.6 46.6 %while.80 = (s32[]{:T(128)}, f32[16,2,512]{2,1,0:T(2,128)S(1)}, f32[16,8,256]{2,1,0:T(8,128)S(1)}, s32[16,8]{1,0:T(8,128)}, s32[16,8,256]{2,1,0:T(8,128)}, /*index=5*/s32[]{:T(128)}) while((s32[]{:T(128)}, f32[16,2,512]{2,1,0:T(2,128)S(1)}, f32[16,8,256]{2,1,0:T(8,128)S(1)}, s32[16,8]{1,0:T(8,128)}, s32[16,8,256]{2,1,0:T(8,128)}, ...), condition=%wide.region_18.19_spmd.clone, body=%wide.region_17.18_spmd.clone.sunk | while | flops 26218528 | bytes 57597 | solution.py:70
  281.1 1.4 fusion.200
  286.9 1.4 fusion.200
  301.5 1.4 fusion.200
  307.3 1.4 fusion.200
  316.0 1.4 fusion.200
  326.3 3.3 all-reduce
  (985 shorter events, 223.9 us)
Async XLA Ops:
  0.6 10.6 %copy-start.2 = (s32[3,32768]{1,0:T(4,128)S(1)}, s32[3,32768]{1,0:T(4,128)}, u32[]{:S(2)}) copy-start(s32[3,32768]{1,0:T(4,128)} %param.36) | copy-start | bytes 1179652
  0.6 10.6 %copy-start.3 = (s32[3,32768]{1,0:T(4,128)S(1)}, s32[3,32768]{1,0:T(4,128)}, u32[]{:S(2)}) copy-start(s32[3,32768]{1,0:T(4,128)} %param.35) | copy-start | bytes 1179652
  35.3 0.7 copy-start.12
  35.3 0.9 copy-start.6
  35.4 1.0 copy-start.7
  38.8 1.0 copy-start.1
  40.8 15.5 %copy-start.11 = (s32[128]{0:T(128)S(1)}, s32[128]{0:T(128)}, u32[]{:S(2)}) copy-start(s32[128]{0:T(128)} %get-tuple-element.730) | copy-start | bytes 1540
  40.8 15.6 %copy-start.10 = (s32[128]{0:T(128)S(1)}, s32[128]{0:T(128)}, u32[]{:S(2)}) copy-start(s32[128]{0:T(128)} %get-tuple-element.731) | copy-start | bytes 1540
  40.8 15.7 %copy-start.9 = (s32[128]{0:T(128)S(1)}, s32[128]{0:T(128)}, u32[]{:S(2)}) copy-start(s32[128]{0:T(128)} %get-tuple-element.634) | copy-start | bytes 1540
  40.8 15.8 %copy-start.8 = (s32[128]{0:T(128)S(1)}, s32[128]{0:T(128)}, u32[]{:S(2)}) copy-start(s32[128]{0:T(128)} %get-tuple-element.636) | copy-start | bytes 1540
  40.8 16.6 %copy-start.5 = (bf16[2,8,16,128]{3,2,0,1:T(8,128)(2,1)S(1)}, bf16[2,8,16,128]{3,2,0,1:T(8,128)(2,1)}, u32[]{:S(2)}) copy-start(bf16[2,8,16,128]{3,2,0,1:T(8,128)(2,1)} %get-tuple-element.727) | copy-start | bytes 196612
  40.8 16.6 %copy-start.4 = (bf16[2,8,16,128]{3,2,0,1:T(8,128)(2,1)S(1)}, bf16[2,8,16,128]{3,2,0,1:T(8,128)(2,1)}, u32[]{:S(2)}) copy-start(bf16[2,8,16,128]{3,2,0,1:T(8,128)(2,1)} %get-tuple-element.729) | copy-start | bytes 196612
  42.3 174.3 %all-to-all-start = ((f32[128,1,5,256]{3,1,2,0:T(1,128)}), f32[128,1,5,256]{3,1,2,0:T(1,128)S(1)}, u32[]{:S(2)}, u32[]{:S(2)}) async-start(f32[128,1,5,256]{3,1,2,0:T(1,128)} %copy.70), calls=%async_computation | async-start | bytes 1310720 | tf_op jit(solution)/shard_map/all_to_all | solution.py:139
  216.5 1.0 copy-start
  219.9 59.5 %all-to-all-start.1 = ((f32[128,1,5,256]{3,1,2,0:T(1,128)}), f32[128,1,5,256]{3,1,2,0:T(1,128)S(1)}, u32[]{:S(2)}, u32[]{:S(2)}) async-start(f32[128,1,5,256]{3,1,2,0:T(1,128)} %copy.77), calls=%async_computation.1 | async-start | bytes 1310720 | tf_op jit(solution)/shard_map/all_to_all | solution.py:139
where the time goes:
time: 339 us; the launch traced here: 333 us
  matrix products  148 us (44%)
  local copies, waits for them, and re-layouts  90.5 us (27%)
  other arithmetic  49.9 us (15%)
  starting transfers between devices  27 us (8%)
  blocking collectives  10.5 us (3%)
  loops' own time  5.3 us (2%)
    dot_general x48, matrix products, deposit_one_bundle(): jnp.einsum('gtw,gwc->tc', weighted, bed_hit, precision=lax.Precision.HIGH...  78.5 us
    dot_general x96, matrix products, interpolate_one_bundle(): jnp.einsum('tqrc,gpc->gtqrp', lookup, column_hit, preferred_element_type=...  69 us
    all_to_all x2, starting transfers between devices, body(): lax.all_to_all(outgoing.reshape(dom_count, per_peer, 5, width), 'dom', sp...  27 us
    select_n x96, other arithmetic, interpolate_one_bundle(): cell_bundle % 128  22.6 us
    eq x96, local copies, waits for them, and re-layouts, interpolate_one_bundle(): tile_hit = (tile_bundle[:, None] == tile_ids[None, :]).astype(jnp.float32)  22.6 us
    eq x48, local copies, waits for them, and re-layouts, deposit_one_bundle(): bed_hit = (bed_bundle[..., None] == bed_ids).astype(jnp.float32)  22.3 us
    eq x48, local copies, waits for them, and re-layouts, deposit_one_bundle(): tile_hit = (tile_bundle[:, None] == tile_ids[None, :]).astype(jnp.float32)  22.2 us
    unnamed x36, local copies, waits for them, and re-layouts  7.41 us
  transfers between devices with their start and end apart: 2, of which 0 were waited for; matrix products, arithmetic and copies ran while one was open for 61% of the time, Pallas kernels for 0%

commit v1 on v0

v1 whole, which is shorter than its diff:
```python
import jax
import jax.numpy as jnp
from jax import lax
from jax.experimental import pallas as pl
from jax.experimental.pallas import tpu as pltpu
from jax.sharding import PartitionSpec as P

NB = 128
WIDTH = 256
PARTS = NB * WIDTH
CELLS = 2048
ROWS = CELLS // 128
BEDC = 512
TILES = 128
DT = 0.5
CHUNK = 32
GROUP = 8

POS_SCALE = 2.0**26
MASS_SCALE = 32767.0
FRAC_SCALE = 166000.0

VMEM = pltpu.VMEM
SMEM = pltpu.SMEM


def whole(space=VMEM):
    return pl.BlockSpec(memory_space=space)


def params():
    return pltpu.CompilerParams(vmem_limit_bytes=40 * 1024 * 1024)


def sublane():
    return lax.broadcasted_iota(jnp.int32, (8, 128), 0)


def fill_tables(tables, own_vel, peer_vel, own_dif, peer_dif, slot, step, arch):
    for vel, dif, tile in ((own_vel, own_dif, arch), (peer_vel, peer_dif, 1 - arch)):
        for c in range(4):
            v = (vel[c] if c < 3 else dif[...]).astype(jnp.float32)
            total = v[step : step + 1] + v[step + 1 : step + 2]
            value = 0.5 * DT * total if c < 3 else jnp.sqrt(DT * total)
            for r in range(ROWS):
                row = value[:, 128 * r : 128 * (r + 1)]
                tables[slot, tile, r, c : c + 1, :] = row
                tables[slot, tile, r, c + 4 : c + 5, :] = row


def halves(low, high, sub):
    return jnp.where(sub < 4, jnp.broadcast_to(low, (8, 128)), jnp.broadcast_to(high, (8, 128)))


def stack_halves(ref, lead, start):
    low = ref[lead + (slice(None), pl.ds(start, 128))]
    high = ref[lead + (slice(None), pl.ds(start + 128, 128))]
    gap = jnp.zeros((1, 128), jnp.float32)
    return jnp.concatenate([low, gap, high, gap], axis=0)


def advance(tables, slot, tile, index, noise, sub):
    lane = index & 127
    values = [
        jnp.take_along_axis(tables[slot, tile, r], lane, axis=1, mode="promise_in_bounds")
        for r in range(ROWS)
    ]
    bit = 128
    while len(values) > 1:
        odd = (index & bit) != 0
        values = [jnp.where(odd, b, a) for a, b in zip(values[0::2], values[1::2])]
        bit *= 2
    value = values[0]
    spread = jnp.where((sub & 3) == 3, value, 0.0)
    spread = spread + pltpu.roll(spread, 7, 0)
    spread = spread + pltpu.roll(spread, 6, 0)
    return value + spread * noise


def cells_of(cell_ref, step, start, sub):
    low = cell_ref[step : step + 1, pl.ds(start, 128)]
    high = cell_ref[step : step + 1, pl.ds(start + 128, 128)]
    return halves(low, high, sub)


def fraction(settling):
    return 1.0 - jnp.exp(-DT * settling)


def first_kernel(
    tile_ref, route_ref, own_vel, peer_vel, own_dif, peer_dif,
    pos_ref, mass_ref, settle_ref, noise_ref, cell_ref, out_ref, tables, code_ref,
):
    arch = lax.axis_index("arch")
    part = pl.program_id(0)

    @pl.when(part == 0)
    def _():
        fill_tables(tables, own_vel, peer_vel, own_dif, peer_dif, 0, 0, arch)

    mass_code = (mass_ref[...] * MASS_SCALE + 0.5).astype(jnp.int32)
    mass_code = jnp.clip(mass_code, 0, 65535) - 32768
    frac_code = (fraction(settle_ref[...]) * FRAC_SCALE + 0.5).astype(jnp.int32)
    frac_code = jnp.clip(frac_code, 0, 65535)
    code_ref[...] = mass_code * 65536 + frac_code
    sub = sublane()
    state_row = (sub & 3) == 3
    fall = jnp.where((sub & 3) == 2, -3.0 * DT, 0.0)

    def block(j, carry):
        start = pl.multiple_of(j * WIDTH, WIDTH)
        slot = part * CHUNK + j
        index = cells_of(cell_ref, 0, start, sub)
        noise = stack_halves(noise_ref, (0,), start)
        here = stack_halves(pos_ref, (), start)
        speed = halves(settle_ref[pl.ds(2 * j, 1), :], settle_ref[pl.ds(2 * j + 1, 1), :], sub)
        here = here + fall * speed
        here = here + advance(tables, 0, tile_ref[0, 0, slot] // TILES, index, noise, sub)
        state = halves(code_ref[pl.ds(2 * j, 1), :], code_ref[pl.ds(2 * j + 1, 1), :], sub)
        code = jnp.where(state_row, state, (here * POS_SCALE).astype(jnp.int32))
        out_ref[route_ref[0, 0, slot]] = code
        return carry

    lax.fori_loop(0, CHUNK, block, 0, unroll=GROUP)


def later_kernel(
    tile_ref, own_vel, peer_vel, own_dif, peer_dif, noise_ref, cell_ref,
    second_ref, third_ref, tables,
):
    arch = lax.axis_index("arch")
    part = pl.program_id(0)

    @pl.when(part == 0)
    def _():
        for step in (1, 2):
            fill_tables(tables, own_vel, peer_vel, own_dif, peer_dif, step - 1, step, arch)

    sub = sublane()
    state_row = (sub & 3) == 3

    def block(j, carry):
        start = pl.multiple_of(j * WIDTH, WIDTH)
        slot = part * CHUNK + j
        for step in (1, 2):
            index = cells_of(cell_ref, step, start, sub)
            noise = stack_halves(noise_ref, (step,), start)
            moved = advance(
                tables, step - 1, tile_ref[step, 0, slot] // TILES, index, noise, sub
            )
            if step == 1:
                code = (moved * POS_SCALE).astype(jnp.int32)
                second_ref[j] = jnp.where(state_row, 0, code)
            else:
                third_ref[j] = moved
        return carry

    lax.fori_loop(0, CHUNK, block, 0, unroll=GROUP // 2)


def relay_kernel(route_ref, in_ref, add_ref, out_ref):
    def block(j, carry):
        out_ref[route_ref[1, 0, j]] = in_ref[j] + add_ref[j]
        return carry

    lax.fori_loop(0, NB, block, 0, unroll=16)


def decode(code):
    mass = ((code >> 16) + 32768).astype(jnp.float32) * (1.0 / MASS_SCALE)
    frac = (code & 65535).astype(jnp.float32) * (1.0 / FRAC_SCALE)
    return mass, frac


def histogram(tile_ref, bed_ref, dep_ref, step):
    sub = sublane()
    lanes = lax.broadcasted_iota(jnp.int32, (128, 128), 0)

    def group(i, total):
        hits = []
        weights = []
        for k in range(GROUP):
            slot = i * GROUP + k
            tile = tile_ref[step, 0, slot] // TILES
            for half in range(2):
                start = pl.multiple_of(slot * WIDTH + half * 128, 128)
                cell = bed_ref[step : step + 1, pl.ds(start, 128)]
                dep = jnp.broadcast_to(dep_ref[pl.ds(2 * slot + half, 1), :], (8, 128))
                cell = jnp.broadcast_to(cell, (8, 128))
                row = (cell >> 7) + tile * 4
                mine = jnp.where(row == sub, dep, 0.0)
                high = mine.astype(jnp.bfloat16).astype(jnp.float32)
                weights.append(jnp.concatenate([high, mine - high], axis=0).astype(jnp.bfloat16))
                column = jnp.broadcast_to((cell & 127)[0:1], (128, 128))
                hits.append(jnp.where(column == lanes, 1.0, 0.0).astype(jnp.bfloat16))
        hit = jnp.concatenate(hits, axis=1)
        weight = jnp.concatenate(weights, axis=1)
        return total + lax.dot_general(
            weight, hit, (((1,), (1,)), ((), ())), preferred_element_type=jnp.float32
        )

    total = lax.fori_loop(0, NB // GROUP, group, jnp.zeros((16, 128), jnp.float32))
    return total[0:8] + total[8:16]


def bed_first_kernel(tile_ref, bed_ref, mass_ref, settle_ref, out_ref, dep_ref):
    dep_ref[...] = mass_ref[...] * fraction(settle_ref[...])
    out_ref[...] = histogram(tile_ref, bed_ref, dep_ref, 0)


def bed_second_kernel(tile_ref, bed_ref, state_ref, before_ref, out_ref, dep_ref):
    mass, frac = decode(state_ref[pl.ds(3, 2 * NB, stride=4), :])
    dep_ref[...] = mass * (1.0 - frac) * frac
    out_ref[...] = before_ref[...] + histogram(tile_ref, bed_ref, dep_ref, 1)


def bed_third_kernel(
    tile_ref, bed_ref, state_ref, before_ref, mass_ref, own_ref, peer_ref, dep_ref
):
    mass, frac = decode(state_ref[pl.ds(3, 2 * NB, stride=4), :])
    left = mass * (1.0 - frac) * (1.0 - frac)
    dep_ref[...] = left * frac
    mass_ref[...] = left * (1.0 - frac)
    total = before_ref[...] + histogram(tile_ref, bed_ref, dep_ref, 2)
    total = total * (BEDC / PARTS)
    first = lax.axis_index("arch") == 0
    own_ref[...] = jnp.where(first, total[0:4], total[4:8])
    peer_ref[...] = jnp.where(first, total[4:8], total[0:4])


def finish_kernel(in_ref, add_ref, out_ref):
    def block(j, carry):
        start = pl.multiple_of(j * WIDTH, WIDTH)
        here = in_ref[j].astype(jnp.float32) * (1.0 / POS_SCALE) + add_ref[j]
        out_ref[:, pl.ds(start, 128)] = here[0:3]
        out_ref[:, pl.ds(start + 128, 128)] = here[4:7]
        return carry

    lax.fori_loop(0, NB, block, 0, unroll=GROUP)


def body(
    position, particle_mass, settling, walk_noise, velocity, diffusivity,
    block_tile, cell_index, bed_cell, route_code,
):
    slabs = velocity.shape[0]
    swap = [(0, 1), (1, 0)]
    vel = velocity.transpose(1, 2, 0, 3).reshape(3, slabs, CELLS)
    dif = diffusivity.transpose(1, 0, 2).reshape(slabs, CELLS)
    peer_vel = lax.ppermute(vel, "arch", swap)
    peer_dif = lax.ppermute(dif, "arch", swap)
    mass = particle_mass.reshape(2 * NB, 128)
    settle = settling.reshape(2 * NB, 128)

    state_type = jax.ShapeDtypeStruct((NB, 8, 128), jnp.int32)
    move_type = jax.ShapeDtypeStruct((NB, 8, 128), jnp.float32)
    bed_type = jax.ShapeDtypeStruct((8, 128), jnp.float32)
    steps = NB // CHUNK
    span = CHUNK * WIDTH
    dep_scratch = [pltpu.VMEM((2 * NB, 128), jnp.float32)]

    outgoing = pl.pallas_call(
        first_kernel,
        grid=(steps,),
        in_specs=[whole(SMEM), whole(SMEM), whole(), whole(), whole(), whole()]
        + [
            pl.BlockSpec((3, span), lambda i: (0, i)),
            pl.BlockSpec((2 * CHUNK, 128), lambda i: (i, 0)),
            pl.BlockSpec((2 * CHUNK, 128), lambda i: (i, 0)),
            pl.BlockSpec((1, 3, span), lambda i: (0, 0, i)),
            pl.BlockSpec((3, span), lambda i: (0, i)),
        ],
        out_specs=pl.BlockSpec((NB, 8, 128), lambda i: (0, 0, 0)),
        out_shape=state_type,
        scratch_shapes=[
            pltpu.VMEM((1, 2, ROWS, 8, 128), jnp.float32),
            pltpu.VMEM((2 * CHUNK, 128), jnp.int32),
        ],
        compiler_params=params(),
        name="first",
    )(
        block_tile, route_code, vel, peer_vel, dif, peer_dif,
        position, mass, settle, walk_noise, cell_index,
    )

    incoming = lax.all_to_all(outgoing, "dom", 0, 0, tiled=True)

    second, third = pl.pallas_call(
        later_kernel,
        grid=(steps,),
        in_specs=[whole(SMEM), whole(), whole(), whole(), whole()]
        + [
            pl.BlockSpec((3, 3, span), lambda i: (0, 0, i)),
            pl.BlockSpec((3, span), lambda i: (0, i)),
        ],
        out_specs=[pl.BlockSpec((CHUNK, 8, 128), lambda i: (i, 0, 0))] * 2,
        out_shape=[state_type, move_type],
        scratch_shapes=[pltpu.VMEM((2, 2, ROWS, 8, 128), jnp.float32)],
        compiler_params=params(),
        cost_estimate=pl.CostEstimate(flops=10**9, bytes_accessed=10**7, transcendentals=0),
        name="later",
    )(block_tile, vel, peer_vel, dif, peer_dif, walk_noise, cell_index)

    bed = pl.pallas_call(
        bed_first_kernel,
        in_specs=[whole(SMEM), whole(), whole(), whole()],
        out_specs=whole(),
        out_shape=bed_type,
        scratch_shapes=dep_scratch,
        compiler_params=params(),
        cost_estimate=pl.CostEstimate(flops=10**9, bytes_accessed=10**7, transcendentals=0),
        name="bed_first",
    )(block_tile, bed_cell, mass, settle)

    outgoing = pl.pallas_call(
        relay_kernel,
        in_specs=[whole(SMEM), whole(), whole()],
        out_specs=whole(),
        out_shape=state_type,
        compiler_params=params(),
        name="relay",
    )(route_code, incoming, second)

    bed = pl.pallas_call(
        bed_second_kernel,
        in_specs=[whole(SMEM), whole(), whole(), whole()],
        out_specs=whole(),
        out_shape=bed_type,
        scratch_shapes=dep_scratch,
        compiler_params=params(),
        cost_estimate=pl.CostEstimate(flops=10**9, bytes_accessed=10**7, transcendentals=0),
        name="bed_second",
    )(block_tile, bed_cell, incoming.reshape(8 * NB, 128), bed)

    incoming = lax.all_to_all(outgoing, "dom", 0, 0, tiled=True)

    final_mass, own, peer = pl.pallas_call(
        bed_third_kernel,
        in_specs=[whole(SMEM), whole(), whole(), whole()],
        out_specs=[whole(), whole(), whole()],
        out_shape=[
            jax.ShapeDtypeStruct((2 * NB, 128), jnp.float32),
            jax.ShapeDtypeStruct((4, 128), jnp.float32),
            jax.ShapeDtypeStruct((4, 128), jnp.float32),
        ],
        scratch_shapes=dep_scratch,
        compiler_params=params(),
        name="bed_third",
    )(block_tile, bed_cell, incoming.reshape(8 * NB, 128), bed)
    other = lax.ppermute(peer, "arch", swap)

    final_position = pl.pallas_call(
        finish_kernel,
        in_specs=[whole(), whole()],
        out_specs=whole(),
        out_shape=jax.ShapeDtypeStruct((3, PARTS), jnp.float32),
        compiler_params=params(),
        cost_estimate=pl.CostEstimate(flops=10**7, bytes_accessed=10**6, transcendentals=0),
        name="finish",
    )(incoming, third)
    return (
        final_position,
        final_mass.reshape(PARTS),
        (own + other).reshape(1, BEDC),
    )


def solution(mesh):
    one = P(("arch", "dom"))
    two = P(None, ("arch", "dom"))
    rows = P(None, ("arch", "dom"), None)
    return jax.shard_map(
        body,
        mesh=mesh,
        in_specs=(
            two, one, one, P(None, None, ("arch", "dom")),
            P(None, None, ("arch", "dom"), None), rows, rows, two, two, rows,
        ),
        out_specs=(two, one, P(("arch", "dom"), None)),
        check_vma=False,
    )
```

time: 339 us -> 90.5 us (0.27); the launches traced: 333 us -> 89.9 us
  matrix products: 148 us -> 0 us
  local copies, waits for them, and re-layouts: 90.5 us -> 10.1 us
  other arithmetic: 49.9 us -> 0.58 us
  Pallas kernels: 0 us -> 31.9 us
  waiting for transfers between devices: 0.01 us -> 18.4 us
  blocking collectives: 10.5 us -> 0 us
  loops' own time: 5.3 us -> 0 us
    dot_general x146 -> x0, matrix products: 148 us -> none  [the longest x48 78.5 us: deposit_one_bundle(): jnp.einsum('gtw,gwc->tc', weighted, bed_hit, precision=lax.Precision.HIGH...]
    eq x193 -> x0, local copies, waits for them, and re-layouts: 67.2 us -> none  [the longest x96 22.6 us: interpolate_one_bundle(): tile_hit = (tile_bundle[:, None] == tile_ids[None, :]).astype(jnp.float32)]
    pallas_call x0 -> x7, Pallas kernels: none -> 31.9 us  [the longest x1 8.75 us: body(): pl.pallas_call(later_kernel, grid=(steps,), in_specs=[whole(SMEM), whole(...]
    select_n x102 -> x0, other arithmetic: 24.5 us -> none  [the longest x96 22.6 us: interpolate_one_bundle(): cell_bundle % 128]
    all_to_all x2, waiting for transfers between devices: 0.01 us -> 17.1 us  [body(): incoming = lax.all_to_all(outgoing, 'dom', 0, 0, tiled=True)]
    convert_element_type x240 -> x0, other arithmetic: 11.3 us -> none  [the longest x96 6.89 us: interpolate_one_bundle(): tile_hit = (tile_bundle[:, None] == tile_ids[None, :]).astype(jnp.float32)]
    mul x103 -> x0, other arithmetic: 9.27 us -> none  [the longest x96 7.39 us: interpolate_one_bundle(): joint = tile_hit[:, :, None, None] * row_hit[:, None]]
    ppermute x0 -> x3, starting transfers between devices: none -> 7.85 us  [the longest x1 4.42 us: body(): other = lax.ppermute(peer, 'arch', swap)]
  transfers between devices with their start and end apart: 2 -> 5, of which waited for: 0 -> 3; matrix products, arithmetic and copies ran while one was open for 61% -> 0% of each run, Pallas kernels for 0% -> 21%
where the time goes in v1:
time: 90.5 us; the launch traced here: 89.9 us
  Pallas kernels  31.9 us (35%)
  starting transfers between devices  28.2 us (31%)
  waiting for transfers between devices  18.4 us (20%)
  local copies, waits for them, and re-layouts  10.1 us (11%)
    all_to_all x2, starting transfers between devices, body(): incoming = lax.all_to_all(outgoing, 'dom', 0, 0, tiled=True)  20.4 us
    all_to_all x2, waiting for transfers between devices, body(): incoming = lax.all_to_all(outgoing, 'dom', 0, 0, tiled=True)  17.1 us
    unnamed x40, local copies, waits for them, and re-layouts  10.1 us
    pallas_call x1, Pallas kernels, body(): pl.pallas_call(later_kernel, grid=(steps,), in_specs=[whole(SMEM), whole(...  8.75 us
    pallas_call x1, Pallas kernels, body(): pl.pallas_call(first_kernel, grid=(steps,), in_specs=[whole(SMEM), whole(...  5.65 us
    pallas_call x1, Pallas kernels, body(): pl.pallas_call(bed_third_kernel, in_specs=[whole(SMEM), whole(), whole(),...  5.2 us
    pallas_call x1, Pallas kernels, body(): pl.pallas_call(bed_second_kernel, in_specs=[whole(SMEM), whole(), whole()...  4.72 us
    pallas_call x1, Pallas kernels, body(): pl.pallas_call(bed_first_kernel, in_specs=[whole(SMEM), whole(), whole(),...  4.69 us
  transfers between devices with their start and end apart: 5, of which 3 were waited for; matrix products, arithmetic and copies ran while one was open for 0% of the time, Pallas kernels for 21%

profile of v1, /device:TPU:1, one launch (start us, length us, event | category | flops | bytes accessed | tf_op | source)
XLA Modules:
  0.0 89.9 jit_solution(8211110632396637141)
XLA Ops:
  0.6 3.3 %collective-permute-start = (bf16[3,4,2048]{2,1,0:T(4,128)(2,1)}, bf16[3,4,2048]{2,1,0:T(4,128)(2,1)S(1)}, u32[]{:S(2)}, u32[]{:S(2)}) collective-permute-start(bf16[3,4,2048]{2,1,0:T(4,128)(2,1)} %bitcast.18), channel_id=1, source_target_pairs={{0,128},{128,0},{1,129},{129,1},{2,130},{130,2},{3,131},{131,3},{4... | collective-permute-start | bytes 147464 | tf_op jit(solution)/shard_map/ppermute | solution.py:250
  4.0 0.1 collective-permute-start.1
  4.1 1.3 %collective-permute-done.1.peer_dif = bf16[4,2048]{1,0:T(4,128)(2,1)S(1)} collective-permute-done((bf16[4,2048]{1,0:T(4,128)(2,1)}, bf16[4,2048]{1,0:T(4,128)(2,1)S(1)}, u32[]{:S(2)}, u32[]{:S(2)}) %collective-permute-start.1) | collective-permute-done | bytes 16416 | tf_op jit(solution)/shard_map/ppermute | solution.py:251
  5.4 0.0 collective-permute-done.peer_vel
  5.4 0.0 copy-start
  5.4 1.4 %copy-done = f32[3,3,32768]{2,1,0:T(4,128)S(1)} copy-done((f32[3,3,32768]{2,1,0:T(4,128)S(1)}, f32[3,3,32768]{2,1,0:T(4,128)}, u32[]{:S(2)}) %copy-start) | copy-done | bytes 1179672
  6.8 0.0 copy-start.2
  6.8 1.0 %copy-done.2 = f32[3,32768]{1,0:T(4,128)S(1)} copy-done((f32[3,32768]{1,0:T(4,128)S(1)}, f32[3,32768]{1,0:T(4,128)}, u32[]{:S(2)}) %copy-start.2) | copy-done | bytes 393240
  7.8 0.0 copy-start.3
  7.8 1.0 %copy-done.3 = s32[3,32768]{1,0:T(4,128)S(1)} copy-done((s32[3,32768]{1,0:T(4,128)S(1)}, s32[3,32768]{1,0:T(4,128)}, u32[]{:S(2)}) %copy-start.3) | copy-done | bytes 393240
  8.9 0.0 copy-start.8
  8.9 0.9 %copy-done.8 = f32[32768]{0:T(1024)S(1)} copy-done((f32[32768]{0:T(1024)S(1)}, f32[32768]{0:T(1024)}, u32[]{:S(2)}) %copy-start.8) | copy-done | bytes 131096
  9.8 0.0 copy-start.10
  9.8 0.9 %copy-done.10 = f32[32768]{0:T(1024)S(1)} copy-done((f32[32768]{0:T(1024)S(1)}, f32[32768]{0:T(1024)}, u32[]{:S(2)}) %copy-start.10) | copy-done | bytes 131096
  10.7 0.8 copy-done.12
  11.5 0.7 copy-done.14
  12.2 0.7 copy-done.16
  12.9 0.7 copy-done.18
  13.6 0.0 copy-start.17
  13.6 5.7 %first.1 = s32[128,8,128]{2,1,0:T(8,128)} custom-call(s32[3,1,128]{2,1,0:T(1,128)S(1)} %copy-done.16, s32[2,1,128]{2,1,0:T(1,128)S(1)} %copy-done.18, bf16[3,4,2048]{2,1,0:T(4,128)(2,1)S(1)} %bitcast.19, bf16[3,4,2048]{2,1,0:T(4,128)(2,1)S(1)} %collective-permute-done.peer_vel, bf16[4,2048]{1,0:T(4,128)(2,1)S(1)} %bitcast.22, ...), custom_call_target="tpu_custom_call" | custom-call | tf_op jit(solution)/shard_map/first/pallas_call | solution.py:262
  19.2 13.8 %all-to-all-start = ((s32[128,8,128]{2,1,0:T(8,128)}), s32[128,8,128]{2,1,0:T(8,128)S(1)}, u32[]{:S(2)}, u32[]{:S(2)}) async-start(s32[128,8,128]{2,1,0:T(8,128)} %first.1), calls=%async_computation | async-start | bytes 1048576 | tf_op jit(solution)/shard_map/all_to_all | solution.py:286
  33.0 0.0 copy-done.1
  33.0 0.0 copy-done.4
  33.0 0.0 copy-done.13
  33.0 0.0 copy-done.15
  33.0 0.0 copy-done.17
  33.0 0.0 copy-start.19
  33.1 0.0 copy-start.9
  33.1 0.0 copy-start.11
  33.1 8.8 %later.1 = (s32[128,8,128]{2,1,0:T(8,128)S(1)}, f32[128,8,128]{2,1,0:T(8,128)S(1)}) custom-call(s32[3,1,128]{2,1,0:T(1,128)S(1)} %copy-done.17, bf16[3,4,2048]{2,1,0:T(4,128)(2,1)S(1)} %bitcast.20, bf16[3,4,2048]{2,1,0:T(4,128)(2,1)S(1)} %collective-permute-done.peer_vel, bf16[4,2048]{1,0:T(4,128)(2,1)S(1)} %bitcast.23, ...), custom_call_target="tpu_custom_call" | custom-call | flops 1000000000 | bytes 10000000 | tf_op jit(solution)/shard_map/later/pallas_call | solution.py:288
  41.8 0.0 copy-start.6
  41.9 0.8 copy-done.6
  42.7 9.4 %all-to-all-done.in_ref = s32[128,8,128]{2,1,0:T(8,128)S(1)} async-done(((s32[128,8,128]{2,1,0:T(8,128)}), s32[128,8,128]{2,1,0:T(8,128)S(1)}, u32[]{:S(2)}, u32[]{:S(2)}) %all-to-all-start) | async-done | bytes 524320 | tf_op jit(solution)/shard_map/all_to_all | solution.py:286
  52.0 0.0 copy-done.19
  52.0 1.0 %copy-done.7 = s32[128,8,128]{2,1,0:T(8,128)S(1)} copy-done((s32[128,8,128]{2,1,0:T(8,128)S(1)}, s32[128,8,128]{2,1,0:T(8,128)}, u32[]{:S(2)}) %copy-start.7) | copy-done | bytes 524312
  53.1 1.7 %relay.1 = s32[128,8,128]{2,1,0:T(8,128)} custom-call(s32[2,1,128]{2,1,0:T(1,128)S(1)} %copy-done.19, s32[128,8,128]{2,1,0:T(8,128)S(1)} %all-to-all-done.in_ref, s32[128,8,128]{2,1,0:T(8,128)S(1)} %copy-done.7), custom_call_target="tpu_custom_call" | custom-call | tf_op jit(solution)/shard_map/relay/pallas_call | solution.py:315
  54.8 6.6 %all-to-all-start.1 = ((s32[128,8,128]{2,1,0:T(8,128)}), s32[128,8,128]{2,1,0:T(8,128)S(1)}, u32[]{:S(2)}, u32[]{:S(2)}) async-start(s32[128,8,128]{2,1,0:T(8,128)} %relay.1), calls=%async_computation.1 | async-start | bytes 1048576 | tf_op jit(solution)/shard_map/all_to_all | solution.py:335
  61.3 0.0 copy-done.9
  61.4 0.0 copy-done.11
  61.4 0.0 copy-done.5
  61.4 4.7 %bed_first.1.before_ref = f32[8,128]{1,0:T(8,128)S(1)} custom-call(s32[3,1,128]{2,1,0:T(1,128)S(1)} %copy-done.17, s32[3,32768]{1,0:T(4,128)S(1)} %copy-done.5, f32[256,128]{1,0:T(8,128)S(1)} %bitcast.15, f32[256,128]{1,0:T(8,128)S(1)} %bitcast.17), custom_call_target="tpu_custom_call" | custom-call | flops 1000000000 | bytes 10000000 | tf_op jit(solution)/shard_map/bed_first/pallas_call | solution.py:304
  66.1 4.7 %bed_second.1.before_ref = f32[8,128]{1,0:T(8,128)S(1)} custom-call(s32[3,1,128]{2,1,0:T(1,128)S(1)} %copy-done.17, s32[3,32768]{1,0:T(4,128)S(1)} %copy-done.5, s32[1024,128]{1,0:T(8,128)S(1)} %bitcast.13, f32[8,128]{1,0:T(8,128)S(1)} %bed_first.1.before_ref), custom_call_target="tpu_custom_call" | custom-call | flops 1000000000 | bytes 10000000 | tf_op jit(solution)/shard_map/bed_second/pallas_call | solution.py:324
  70.8 7.8 %all-to-all-done.1.in_ref = s32[128,8,128]{2,1,0:T(8,128)S(1)} async-done(((s32[128,8,128]{2,1,0:T(8,128)}), s32[128,8,128]{2,1,0:T(8,128)S(1)}, u32[]{:S(2)}, u32[]{:S(2)}) %all-to-all-start.1) | async-done | bytes 524320 | tf_op jit(solution)/shard_map/all_to_all | solution.py:335
  78.5 5.2 %bed_third.1 = (f32[256,128]{1,0:T(8,128)}, f32[4,128]{1,0:T(4,128)S(1)}, f32[4,128]{1,0:T(4,128)S(1)}) custom-call(s32[3,1,128]{2,1,0:T(1,128)S(1)} %copy-done.17, s32[3,32768]{1,0:T(4,128)S(1)} %copy-done.5, s32[1024,128]{1,0:T(8,128)S(1)} %bitcast.12, f32[8,128]{1,0:T(8,128)S(1)} %bed_second.1.before_ref), custom_call_target="tpu_custom_call" | custom-call | tf_op jit(solution)/shard_map/bed_third/pallas_call | solution.py:337
  83.7 4.4 %collective-permute-start.2 = (f32[4,128]{1,0:T(4,128)S(1)}, f32[4,128]{1,0:T(4,128)S(1)}, u32[]{:S(2)}, u32[]{:S(2)}) collective-permute-start(f32[4,128]{1,0:T(4,128)S(1)} %get-tuple-element.12), channel_id=1, source_target_pairs={{0,128},{128,0},{1,129},{129,1},{2,130},{130,2},{3,131},{131,3},{4... | collective-permute-start | bytes 6152 | tf_op jit(solution)/shard_map/ppermute | solution.py:350
  88.2 1.2 %finish.1 = f32[3,32768]{1,0:T(4,128)} custom-call(s32[128,8,128]{2,1,0:T(8,128)S(1)} %all-to-all-done.1.in_ref, f32[128,8,128]{2,1,0:T(8,128)S(1)} %get-tuple-element.9.add_ref), custom_call_target="tpu_custom_call" | custom-call | flops 10000000 | bytes 1000000 | tf_op jit(solution)/shard_map/finish/pallas_call | solution.py:352
  89.3 0.0 collective-permute-done.2
  89.3 0.6 add.3
  (10 shorter events, 0.0 us)
Async XLA Ops:
  0.6 4.7 %collective-permute-start = (bf16[3,4,2048]{2,1,0:T(4,128)(2,1)}, bf16[3,4,2048]{2,1,0:T(4,128)(2,1)S(1)}, u32[]{:S(2)}, u32[]{:S(2)}) collective-permute-start(bf16[3,4,2048]{2,1,0:T(4,128)(2,1)} %bitcast.18), channel_id=1, source_target_pairs={{0,128},{128,0},{1,129},{129,1},{2,130},{130,2},{3,131},{131,3},{4... | collective-permute-start | bytes 147464 | tf_op jit(solution)/shard_map/ppermute | solution.py:250
  4.0 1.4 %collective-permute-start.1 = (bf16[4,2048]{1,0:T(4,128)(2,1)}, bf16[4,2048]{1,0:T(4,128)(2,1)S(1)}, u32[]{:S(2)}, u32[]{:S(2)}) collective-permute-start(bf16[4,2048]{1,0:T(4,128)(2,1)} %bitcast.21), channel_id=1, source_target_pairs={{0,128},{128,0},{1,129},{129,1},{2,130},{130,2},{3,131},{131,3},{4... | collective-permute-start | bytes 49160 | tf_op jit(solution)/shard_map/ppermute | solution.py:251
  5.4 1.4 %copy-start = (f32[3,3,32768]{2,1,0:T(4,128)S(1)}, f32[3,3,32768]{2,1,0:T(4,128)}, u32[]{:S(2)}) copy-start(f32[3,3,32768]{2,1,0:T(4,128)} %noise_ref.3) | copy-start | bytes 3538948
  6.8 1.0 %copy-start.2 = (f32[3,32768]{1,0:T(4,128)S(1)}, f32[3,32768]{1,0:T(4,128)}, u32[]{:S(2)}) copy-start(f32[3,32768]{1,0:T(4,128)} %pos_ref.1) | copy-start | bytes 1179652
  7.8 1.0 %copy-start.3 = (s32[3,32768]{1,0:T(4,128)S(1)}, s32[3,32768]{1,0:T(4,128)}, u32[]{:S(2)}) copy-start(s32[3,32768]{1,0:T(4,128)} %cell_ref.3) | copy-start | bytes 1179652
  8.9 0.9 %copy-start.8 = (f32[32768]{0:T(1024)S(1)}, f32[32768]{0:T(1024)}, u32[]{:S(2)}) copy-start(f32[32768]{0:T(1024)} %param.11) | copy-start | bytes 393220
  9.8 0.9 %copy-start.10 = (f32[32768]{0:T(1024)S(1)}, f32[32768]{0:T(1024)}, u32[]{:S(2)}) copy-start(f32[32768]{0:T(1024)} %param.12) | copy-start | bytes 393220
  10.7 0.8 copy-start.12
  11.5 0.7 copy-start.14
  12.2 0.7 copy-start.16
  12.9 0.7 copy-start.18
  13.5 19.5 %copy-start.1 = (f32[3,3,32768]{2,1,0:T(4,128)S(1)}, f32[3,3,32768]{2,1,0:T(4,128)}, u32[]{:S(2)}) copy-start(f32[3,3,32768]{2,1,0:T(4,128)} %noise_ref.3) | copy-start | bytes 3538948
  13.5 19.5 %copy-start.4 = (s32[3,32768]{1,0:T(4,128)S(1)}, s32[3,32768]{1,0:T(4,128)}, u32[]{:S(2)}) copy-start(s32[3,32768]{1,0:T(4,128)} %cell_ref.3) | copy-start | bytes 1179652
  13.5 19.5 %copy-start.13 = (bf16[4,3,1,2048]{3,0,2,1:T(4,128)(2,1)S(1)}, bf16[4,3,1,2048]{3,0,2,1:T(4,128)(2,1)}, u32[]{:S(2)}) copy-start(bf16[4,3,1,2048]{3,0,2,1:T(4,128)(2,1)} %param.14) | copy-start | bytes 147460
  13.5 19.5 %copy-start.15 = (bf16[4,1,2048]{2,0,1:T(4,128)(2,1)S(1)}, bf16[4,1,2048]{2,0,1:T(4,128)(2,1)}, u32[]{:S(2)}) copy-start(bf16[4,1,2048]{2,0,1:T(4,128)(2,1)} %param.15) | copy-start | bytes 49156
  13.6 19.5 %copy-start.17 = (s32[3,1,128]{2,1,0:T(1,128)S(1)}, s32[3,1,128]{2,1,0:T(1,128)}, u32[]{:S(2)}) copy-start(s32[3,1,128]{2,1,0:T(1,128)} %tile_ref.9) | copy-start | bytes 4612
  19.2 32.8 %all-to-all-start = ((s32[128,8,128]{2,1,0:T(8,128)}), s32[128,8,128]{2,1,0:T(8,128)S(1)}, u32[]{:S(2)}, u32[]{:S(2)}) async-start(s32[128,8,128]{2,1,0:T(8,128)} %first.1), calls=%async_computation | async-start | bytes 1048576 | tf_op jit(solution)/shard_map/all_to_all | solution.py:286
  33.0 19.0 %copy-start.19 = (s32[2,1,128]{2,1,0:T(1,128)S(1)}, s32[2,1,128]{2,1,0:T(1,128)}, u32[]{:S(2)}) copy-start(s32[2,1,128]{2,1,0:T(1,128)} %route_ref.3) | copy-start | bytes 3076
  33.1 28.3 %copy-start.9 = (f32[32768]{0:T(1024)S(1)}, f32[32768]{0:T(1024)}, u32[]{:S(2)}) copy-start(f32[32768]{0:T(1024)} %param.11) | copy-start | bytes 393220
  33.1 28.3 %copy-start.11 = (f32[32768]{0:T(1024)S(1)}, f32[32768]{0:T(1024)}, u32[]{:S(2)}) copy-start(f32[32768]{0:T(1024)} %param.12) | copy-start | bytes 393220
  41.8 0.8 copy-start.6
  42.7 18.7 %copy-start.5 = (s32[3,32768]{1,0:T(4,128)S(1)}, s32[3,32768]{1,0:T(4,128)}, u32[]{:S(2)}) copy-start(s32[3,32768]{1,0:T(4,128)} %bed_ref.5) | copy-start | bytes 1179652
  52.0 1.0 %copy-start.7 = (s32[128,8,128]{2,1,0:T(8,128)S(1)}, s32[128,8,128]{2,1,0:T(8,128)}, u32[]{:S(2)}) copy-start(s32[128,8,128]{2,1,0:T(8,128)} %copy-done.6) | copy-start | bytes 1572868
  54.8 23.8 %all-to-all-start.1 = ((s32[128,8,128]{2,1,0:T(8,128)}), s32[128,8,128]{2,1,0:T(8,128)S(1)}, u32[]{:S(2)}, u32[]{:S(2)}) async-start(s32[128,8,128]{2,1,0:T(8,128)} %relay.1), calls=%async_computation.1 | async-start | bytes 1048576 | tf_op jit(solution)/shard_map/all_to_all | solution.py:335
  83.7 5.6 %collective-permute-start.2 = (f32[4,128]{1,0:T(4,128)S(1)}, f32[4,128]{1,0:T(4,128)S(1)}, u32[]{:S(2)}, u32[]{:S(2)}) collective-permute-start(f32[4,128]{1,0:T(4,128)S(1)} %get-tuple-element.12), channel_id=1, source_target_pairs={{0,128},{128,0},{1,129},{129,1},{2,130},{130,2},{3,131},{131,3},{4... | collective-permute-start | bytes 6152 | tf_op jit(solution)/shard_map/ppermute | solution.py:350

commit v2 on v1

--- a/solution.py
+++ b/solution.py
@@ -13,8 +13,10 @@
 BEDC = 512
 TILES = 128
 DT = 0.5
-CHUNK = 32
-GROUP = 8
+CHUNK = 64
+GROUP = 32
+FIRST_UNROLL = 32
+LATER_UNROLL = 16
 
 POS_SCALE = 2.0**26
 MASS_SCALE = 32767.0
@@ -28,8 +30,16 @@
     return pl.BlockSpec(memory_space=space)
 
 
-def params():
-    return pltpu.CompilerParams(vmem_limit_bytes=40 * 1024 * 1024)
+def params(mebibytes=24):
+    return pltpu.CompilerParams(vmem_limit_bytes=mebibytes * 1024 * 1024)
+
+
+def in_hbm(*arrays):
+    return [pltpu.with_memory_space_constraint(a, pltpu.HBM) for a in arrays]
+
+
+def in_vmem(kind):
+    return pltpu.VMEM(kind.shape, kind.dtype)
 
 
 def sublane():
@@ -121,7 +131,7 @@
         out_ref[route_ref[0, 0, slot]] = code
         return carry
 
-    lax.fori_loop(0, CHUNK, block, 0, unroll=GROUP)
+    lax.fori_loop(0, CHUNK, block, 0, unroll=FIRST_UNROLL)
 
 
 def later_kernel(
@@ -155,7 +165,7 @@
                 third_ref[j] = moved
         return carry
 
-    lax.fori_loop(0, CHUNK, block, 0, unroll=GROUP // 2)
+    lax.fori_loop(0, CHUNK, block, 0, unroll=LATER_UNROLL)
 
 
 def relay_kernel(route_ref, in_ref, add_ref, out_ref):
@@ -236,7 +246,7 @@
         out_ref[:, pl.ds(start + 128, 128)] = here[4:7]
         return carry
 
-    lax.fori_loop(0, NB, block, 0, unroll=GROUP)
+    lax.fori_loop(0, NB, block, 0, unroll=16)
 
 
 def body(
@@ -279,8 +289,8 @@
         compiler_params=params(),
         name="first",
     )(
-        block_tile, route_code, vel, peer_vel, dif, peer_dif,
-        position, mass, settle, walk_noise, cell_index,
+        *in_hbm(block_tile, route_code), *in_hbm(vel), peer_vel, *in_hbm(dif), peer_dif,
+        *in_hbm(position, mass, settle, walk_noise, cell_index),
     )
 
     incoming = lax.all_to_all(outgoing, "dom", 0, 0, tiled=True)
@@ -294,12 +304,12 @@
             pl.BlockSpec((3, span), lambda i: (0, i)),
         ],
         out_specs=[pl.BlockSpec((CHUNK, 8, 128), lambda i: (i, 0, 0))] * 2,
-        out_shape=[state_type, move_type],
+        out_shape=[in_vmem(state_type), in_vmem(move_type)],
         scratch_shapes=[pltpu.VMEM((2, 2, ROWS, 8, 128), jnp.float32)],
         compiler_params=params(),
         cost_estimate=pl.CostEstimate(flops=10**9, bytes_accessed=10**7, transcendentals=0),
         name="later",
-    )(block_tile, vel, peer_vel, dif, peer_dif, walk_noise, cell_index)
+    )(*in_hbm(block_tile, vel), peer_vel, *in_hbm(dif), peer_dif, *in_hbm(walk_noise, cell_index))
 
     bed = pl.pallas_call(
         bed_first_kernel,

time: 90.5 us -> 78.9 us (0.87)
  local copies, waits for them, and re-layouts: 10.1 us -> 0.03 us
  Pallas kernels: 31.9 us -> 25.5 us
  waiting for transfers between devices: 18.4 us -> 23.6 us
    unnamed x40 -> x10, local copies, waits for them, and re-layouts: 10.1 us -> 0.03 us
    all_to_all x2, waiting for transfers between devices: 17.1 us -> 22.3 us  [body(): incoming = lax.all_to_all(outgoing, 'dom', 0, 0, tiled=True)]
    pallas_call x1, Pallas kernels: 8.75 us -> 7.26 us  [body(): pl.pallas_call(later_kernel, grid=(steps,), in_specs=[whole(SMEM), whole(...]
    pallas_call x1, Pallas kernels: 4.69 us -> 3.24 us  [body(): pl.pallas_call(bed_first_kernel, in_specs=[whole(SMEM), whole(), whole(),...]
    pallas_call x1, Pallas kernels: 4.72 us -> 3.27 us  [body(): pl.pallas_call(bed_second_kernel, in_specs=[whole(SMEM), whole(), whole()...]
    pallas_call x1, Pallas kernels: 5.2 us -> 3.77 us  [body(): pl.pallas_call(bed_third_kernel, in_specs=[whole(SMEM), whole(), whole(),...]
  transfers between devices with their start and end apart: 5 -> 5, of which waited for: 3 -> 3; matrix products, arithmetic and copies ran while one was open for 0% -> 0% of each run, Pallas kernels for 21% -> 19%
where the time goes in v2:
time: 78.9 us; the launch traced here: 78.7 us
  starting transfers between devices  28.2 us (36%)
  Pallas kernels  25.5 us (32%)
  waiting for transfers between devices  23.6 us (30%)
    all_to_all x2, waiting for transfers between devices, body(): incoming = lax.all_to_all(outgoing, 'dom', 0, 0, tiled=True)  22.3 us
    all_to_all x2, starting transfers between devices, body(): incoming = lax.all_to_all(outgoing, 'dom', 0, 0, tiled=True)  20.4 us
    pallas_call x1, Pallas kernels, body(): pl.pallas_call(later_kernel, grid=(steps,), in_specs=[whole(SMEM), whole(...  7.26 us
    pallas_call x1, Pallas kernels, body(): pl.pallas_call(first_kernel, grid=(steps,), in_specs=[whole(SMEM), whole(...  5.16 us
    ppermute x1, starting transfers between devices, body(): other = lax.ppermute(peer, 'arch', swap)  4.42 us
    pallas_call x1, Pallas kernels, body(): pl.pallas_call(bed_third_kernel, in_specs=[whole(SMEM), whole(), whole(),...  3.77 us
    ppermute x1, starting transfers between devices, body(): peer_vel = lax.ppermute(vel, 'arch', swap)  3.33 us
    pallas_call x1, Pallas kernels, body(): pl.pallas_call(bed_second_kernel, in_specs=[whole(SMEM), whole(), whole()...  3.27 us
  transfers between devices with their start and end apart: 5, of which 3 were waited for; matrix products, arithmetic and copies ran while one was open for 0% of the time, Pallas kernels for 19%

profile of v2, /device:TPU:1, one launch (start us, length us, event | category | flops | bytes accessed | tf_op | source)
XLA Modules:
  0.0 78.7 jit_solution(15747208372186874129)
XLA Ops:
  0.6 3.3 %collective-permute-start = (bf16[3,4,2048]{2,1,0:T(4,128)(2,1)}, bf16[3,4,2048]{2,1,0:T(4,128)(2,1)S(1)}, u32[]{:S(2)}, u32[]{:S(2)}) collective-permute-start(bf16[3,4,2048]{2,1,0:T(4,128)(2,1)} %bitcast.18), channel_id=1, source_target_pairs={{0,128},{128,0},{1,129},{129,1},{2,130},{130,2},{3,131},{131,3},{4... | collective-permute-start | bytes 147464 | tf_op jit(solution)/shard_map/ppermute | solution.py:260
  4.0 0.1 collective-permute-start.1
  4.1 1.3 %collective-permute-done.1.peer_dif = bf16[4,2048]{1,0:T(4,128)(2,1)S(1)} collective-permute-done((bf16[4,2048]{1,0:T(4,128)(2,1)}, bf16[4,2048]{1,0:T(4,128)(2,1)S(1)}, u32[]{:S(2)}, u32[]{:S(2)}) %collective-permute-start.1) | collective-permute-done | bytes 16416 | tf_op jit(solution)/shard_map/ppermute | solution.py:261
  5.4 0.0 collective-permute-done.peer_vel
  5.4 5.2 %first.1 = s32[128,8,128]{2,1,0:T(8,128)} custom-call(s32[3,1,128]{2,1,0:T(1,128)} %tile_ref.9, s32[2,1,128]{2,1,0:T(1,128)} %route_ref.3, bf16[3,4,2048]{2,1,0:T(4,128)(2,1)} %bitcast.19, bf16[3,4,2048]{2,1,0:T(4,128)(2,1)S(1)} %collective-permute-done.peer_vel, bf16[4,2048]{1,0:T(4,128)(2,1)} %bitcast.22, ...), custom_call_target="tpu_custom_call" | custom-call | tf_op jit(solution)/shard_map/first/pallas_call | solution.py:272
  10.5 13.8 %all-to-all-start = ((s32[128,8,128]{2,1,0:T(8,128)}), s32[128,8,128]{2,1,0:T(8,128)S(1)}, u32[]{:S(2)}, u32[]{:S(2)}) async-start(s32[128,8,128]{2,1,0:T(8,128)} %first.1), calls=%async_computation | async-start | bytes 1048576 | tf_op jit(solution)/shard_map/all_to_all | solution.py:296
  24.3 0.0 copy-start.4
  24.3 7.3 %later.1 = (s32[128,8,128]{2,1,0:T(8,128)S(1)}, f32[128,8,128]{2,1,0:T(8,128)S(1)}) custom-call(s32[3,1,128]{2,1,0:T(1,128)} %tile_ref.9, bf16[3,4,2048]{2,1,0:T(4,128)(2,1)} %bitcast.20, bf16[3,4,2048]{2,1,0:T(4,128)(2,1)S(1)} %collective-permute-done.peer_vel, bf16[4,2048]{1,0:T(4,128)(2,1)} %bitcast.23, ...), custom_call_target="tpu_custom_call" | custom-call | flops 1000000000 | bytes 10000000 | tf_op jit(solution)/shard_map/later/pallas_call | solution.py:298
  31.6 0.0 copy-start
  31.6 0.0 copy-start.1
  31.6 0.0 copy-start.2
  31.6 0.0 copy-start.3
  31.6 11.7 %all-to-all-done.in_ref = s32[128,8,128]{2,1,0:T(8,128)S(1)} async-done(((s32[128,8,128]{2,1,0:T(8,128)}), s32[128,8,128]{2,1,0:T(8,128)S(1)}, u32[]{:S(2)}, u32[]{:S(2)}) %all-to-all-start) | async-done | bytes 524320 | tf_op jit(solution)/shard_map/all_to_all | solution.py:296
  43.3 0.0 copy-done.4
  43.3 1.7 %relay.1 = s32[128,8,128]{2,1,0:T(8,128)} custom-call(s32[2,1,128]{2,1,0:T(1,128)S(1)} %copy-done.4, s32[128,8,128]{2,1,0:T(8,128)S(1)} %all-to-all-done.in_ref, s32[128,8,128]{2,1,0:T(8,128)S(1)} %get-tuple-element.8.add_ref), custom_call_target="tpu_custom_call" | custom-call | tf_op jit(solution)/shard_map/relay/pallas_call | solution.py:325
  45.0 6.6 %all-to-all-start.1 = ((s32[128,8,128]{2,1,0:T(8,128)}), s32[128,8,128]{2,1,0:T(8,128)S(1)}, u32[]{:S(2)}, u32[]{:S(2)}) async-start(s32[128,8,128]{2,1,0:T(8,128)} %relay.1), calls=%async_computation.1 | async-start | bytes 1048576 | tf_op jit(solution)/shard_map/all_to_all | solution.py:345
  51.6 0.0 copy-done
  51.6 0.0 copy-done.1
  51.6 0.0 copy-done.2
  51.6 0.0 copy-done.3
  51.6 3.2 %bed_first.1.before_ref = f32[8,128]{1,0:T(8,128)S(1)} custom-call(s32[3,1,128]{2,1,0:T(1,128)S(1)} %copy-done.3, s32[3,32768]{1,0:T(4,128)S(1)} %copy-done, f32[256,128]{1,0:T(8,128)S(1)} %bitcast.15, f32[256,128]{1,0:T(8,128)S(1)} %bitcast.17), custom_call_target="tpu_custom_call" | custom-call | flops 1000000000 | bytes 10000000 | tf_op jit(solution)/shard_map/bed_first/pallas_call | solution.py:314
  54.9 3.3 %bed_second.1.before_ref = f32[8,128]{1,0:T(8,128)S(1)} custom-call(s32[3,1,128]{2,1,0:T(1,128)S(1)} %copy-done.3, s32[3,32768]{1,0:T(4,128)S(1)} %copy-done, s32[1024,128]{1,0:T(8,128)S(1)} %bitcast.13, f32[8,128]{1,0:T(8,128)S(1)} %bed_first.1.before_ref), custom_call_target="tpu_custom_call" | custom-call | flops 1000000000 | bytes 10000000 | tf_op jit(solution)/shard_map/bed_second/pallas_call | solution.py:334
  58.2 10.6 %all-to-all-done.1.in_ref = s32[128,8,128]{2,1,0:T(8,128)S(1)} async-done(((s32[128,8,128]{2,1,0:T(8,128)}), s32[128,8,128]{2,1,0:T(8,128)S(1)}, u32[]{:S(2)}, u32[]{:S(2)}) %all-to-all-start.1) | async-done | bytes 524320 | tf_op jit(solution)/shard_map/all_to_all | solution.py:345
  68.8 3.8 %bed_third.1 = (f32[256,128]{1,0:T(8,128)}, f32[4,128]{1,0:T(4,128)S(1)}, f32[4,128]{1,0:T(4,128)S(1)}) custom-call(s32[3,1,128]{2,1,0:T(1,128)S(1)} %copy-done.3, s32[3,32768]{1,0:T(4,128)S(1)} %copy-done, s32[1024,128]{1,0:T(8,128)S(1)} %bitcast.12, f32[8,128]{1,0:T(8,128)S(1)} %bed_second.1.before_ref), custom_call_target="tpu_custom_call" | custom-call | tf_op jit(solution)/shard_map/bed_third/pallas_call | solution.py:347
  72.6 4.4 %collective-permute-start.2 = (f32[4,128]{1,0:T(4,128)S(1)}, f32[4,128]{1,0:T(4,128)S(1)}, u32[]{:S(2)}, u32[]{:S(2)}) collective-permute-start(f32[4,128]{1,0:T(4,128)S(1)} %get-tuple-element.12), channel_id=1, source_target_pairs={{0,128},{128,0},{1,129},{129,1},{2,130},{130,2},{3,131},{131,3},{4... | collective-permute-start | bytes 6152 | tf_op jit(solution)/shard_map/ppermute | solution.py:360
  77.0 1.1 %finish.1 = f32[3,32768]{1,0:T(4,128)} custom-call(s32[128,8,128]{2,1,0:T(8,128)S(1)} %all-to-all-done.1.in_ref, f32[128,8,128]{2,1,0:T(8,128)S(1)} %get-tuple-element.9.add_ref), custom_call_target="tpu_custom_call" | custom-call | flops 10000000 | bytes 1000000 | tf_op jit(solution)/shard_map/finish/pallas_call | solution.py:362
  78.1 0.0 collective-permute-done.2
  78.1 0.6 add.3
Async XLA Ops:
  0.6 4.7 %collective-permute-start = (bf16[3,4,2048]{2,1,0:T(4,128)(2,1)}, bf16[3,4,2048]{2,1,0:T(4,128)(2,1)S(1)}, u32[]{:S(2)}, u32[]{:S(2)}) collective-permute-start(bf16[3,4,2048]{2,1,0:T(4,128)(2,1)} %bitcast.18), channel_id=1, source_target_pairs={{0,128},{128,0},{1,129},{129,1},{2,130},{130,2},{3,131},{131,3},{4... | collective-permute-start | bytes 147464 | tf_op jit(solution)/shard_map/ppermute | solution.py:260
  4.0 1.4 %collective-permute-start.1 = (bf16[4,2048]{1,0:T(4,128)(2,1)}, bf16[4,2048]{1,0:T(4,128)(2,1)S(1)}, u32[]{:S(2)}, u32[]{:S(2)}) collective-permute-start(bf16[4,2048]{1,0:T(4,128)(2,1)} %bitcast.21), channel_id=1, source_target_pairs={{0,128},{128,0},{1,129},{129,1},{2,130},{130,2},{3,131},{131,3},{4... | collective-permute-start | bytes 49160 | tf_op jit(solution)/shard_map/ppermute | solution.py:261
  10.5 32.8 %all-to-all-start = ((s32[128,8,128]{2,1,0:T(8,128)}), s32[128,8,128]{2,1,0:T(8,128)S(1)}, u32[]{:S(2)}, u32[]{:S(2)}) async-start(s32[128,8,128]{2,1,0:T(8,128)} %first.1), calls=%async_computation | async-start | bytes 1048576 | tf_op jit(solution)/shard_map/all_to_all | solution.py:296
  24.3 19.0 %copy-start.4 = (s32[2,1,128]{2,1,0:T(1,128)S(1)}, s32[2,1,128]{2,1,0:T(1,128)}, u32[]{:S(2)}) copy-start(s32[2,1,128]{2,1,0:T(1,128)} %route_ref.3) | copy-start | bytes 3076
  31.6 20.0 %copy-start = (s32[3,32768]{1,0:T(4,128)S(1)}, s32[3,32768]{1,0:T(4,128)}, u32[]{:S(2)}) copy-start(s32[3,32768]{1,0:T(4,128)} %bed_ref.5) | copy-start | bytes 1179652
  31.6 20.0 %copy-start.1 = (f32[32768]{0:T(1024)S(1)}, f32[32768]{0:T(1024)}, u32[]{:S(2)}) copy-start(f32[32768]{0:T(1024)} %param.11) | copy-start | bytes 393220
  31.6 20.0 %copy-start.2 = (f32[32768]{0:T(1024)S(1)}, f32[32768]{0:T(1024)}, u32[]{:S(2)}) copy-start(f32[32768]{0:T(1024)} %param.12) | copy-start | bytes 393220
  31.6 20.0 %copy-start.3 = (s32[3,1,128]{2,1,0:T(1,128)S(1)}, s32[3,1,128]{2,1,0:T(1,128)}, u32[]{:S(2)}) copy-start(s32[3,1,128]{2,1,0:T(1,128)} %tile_ref.9) | copy-start | bytes 4612
  45.0 23.8 %all-to-all-start.1 = ((s32[128,8,128]{2,1,0:T(8,128)}), s32[128,8,128]{2,1,0:T(8,128)S(1)}, u32[]{:S(2)}, u32[]{:S(2)}) async-start(s32[128,8,128]{2,1,0:T(8,128)} %relay.1), calls=%async_computation.1 | async-start | bytes 1048576 | tf_op jit(solution)/shard_map/all_to_all | solution.py:345
  72.6 5.5 %collective-permute-start.2 = (f32[4,128]{1,0:T(4,128)S(1)}, f32[4,128]{1,0:T(4,128)S(1)}, u32[]{:S(2)}, u32[]{:S(2)}) collective-permute-start(f32[4,128]{1,0:T(4,128)S(1)} %get-tuple-element.12), channel_id=1, source_target_pairs={{0,128},{128,0},{1,129},{129,1},{2,130},{130,2},{3,131},{131,3},{4... | collective-permute-start | bytes 6152 | tf_op jit(solution)/shard_map/ppermute | solution.py:360

commit v3 on v2

--- a/solution.py
+++ b/solution.py
@@ -182,56 +182,79 @@
     return mass, frac
 
 
-def histogram(tile_ref, bed_ref, dep_ref, step):
-    sub = sublane()
-    lanes = lax.broadcasted_iota(jnp.int32, (128, 128), 0)
+def split_cells(tile_ref, bed_ref, step, row_ref, column_ref):
+    def block(slot, carry):
+        tile = tile_ref[step, 0, slot] // TILES
+        for half in range(2):
+            start = pl.multiple_of(slot * WIDTH + half * 128, 128)
+            cell = bed_ref[step : step + 1, pl.ds(start, 128)]
+            run = pl.ds(2 * slot + half, 1)
+            row_ref[run, :] = ((cell >> 6) + tile * 8).astype(jnp.float32)
+            column_ref[run, :] = (cell & 63).astype(jnp.float32)
+        return carry
+
+    lax.fori_loop(0, NB, block, 0, unroll=16)
+
+
+def spread_run(ref, run):
+    row = jnp.broadcast_to(ref[pl.ds(run, 1), :], (8, 128))
+    return jnp.concatenate([row, row], axis=0).astype(jnp.bfloat16)
+
+
+def histogram(row_ref, column_ref, dep, high_ref, rest_ref, lay_ref):
+    high = dep.astype(jnp.bfloat16).astype(jnp.float32)
+    high_ref[...] = high
+    rest_ref[...] = dep - high
+    places = lax.broadcasted_iota(jnp.int32, (64, 128), 0).astype(jnp.float32).astype(jnp.bfloat16)
+    one, zero = jnp.bfloat16(1), jnp.bfloat16(0)
 
     def group(i, total):
         hits = []
         weights = []
-        for k in range(GROUP):
-            slot = i * GROUP + k
-            tile = tile_ref[step, 0, slot] // TILES
-            for half in range(2):
-                start = pl.multiple_of(slot * WIDTH + half * 128, 128)
-                cell = bed_ref[step : step + 1, pl.ds(start, 128)]
-                dep = jnp.broadcast_to(dep_ref[pl.ds(2 * slot + half, 1), :], (8, 128))
-                cell = jnp.broadcast_to(cell, (8, 128))
-                row = (cell >> 7) + tile * 4
-                mine = jnp.where(row == sub, dep, 0.0)
-                high = mine.astype(jnp.bfloat16).astype(jnp.float32)
-                weights.append(jnp.concatenate([high, mine - high], axis=0).astype(jnp.bfloat16))
-                column = jnp.broadcast_to((cell & 127)[0:1], (128, 128))
-                hits.append(jnp.where(column == lanes, 1.0, 0.0).astype(jnp.bfloat16))
+        for k in range(2 * GROUP):
+            run = 2 * GROUP * i + k
+            mine = spread_run(row_ref, run) == places[0:16]
+            parts = [jnp.where(mine, spread_run(ref, run), zero) for ref in (high_ref, rest_ref)]
+            weights.append(jnp.concatenate(parts, axis=0))
+            column = jnp.concatenate([spread_run(column_ref, run)] * 4, axis=0)
+            hits.append(jnp.where(column == places, one, zero))
+        weight = jnp.concatenate(weights, axis=1)
         hit = jnp.concatenate(hits, axis=1)
-        weight = jnp.concatenate(weights, axis=1)
         return total + lax.dot_general(
             weight, hit, (((1,), (1,)), ((), ())), preferred_element_type=jnp.float32
         )
 
-    total = lax.fori_loop(0, NB // GROUP, group, jnp.zeros((16, 128), jnp.float32))
-    return total[0:8] + total[8:16]
-
-
-def bed_first_kernel(tile_ref, bed_ref, mass_ref, settle_ref, out_ref, dep_ref):
-    dep_ref[...] = mass_ref[...] * fraction(settle_ref[...])
-    out_ref[...] = histogram(tile_ref, bed_ref, dep_ref, 0)
-
-
-def bed_second_kernel(tile_ref, bed_ref, state_ref, before_ref, out_ref, dep_ref):
+    total = lax.fori_loop(0, NB // GROUP, group, jnp.zeros((32, 64), jnp.float32), unroll=4)
+    lay_ref[:, 0:64] = total[0:16] + total[16:32]
+    return jnp.concatenate([lay_ref[pl.ds(i, 8, stride=2), 0:64] for i in range(2)], axis=1)
+
+
+def bed_first_kernel(
+    tile_ref, bed_ref, mass_ref, settle_ref, out_ref, row_ref, column_ref, *scratch
+):
+    split_cells(tile_ref, bed_ref, 0, row_ref, column_ref)
+    dep = mass_ref[...] * fraction(settle_ref[...])
+    out_ref[...] = histogram(row_ref, column_ref, dep, *scratch)
+
+
+def bed_second_kernel(
+    tile_ref, bed_ref, state_ref, before_ref, out_ref, next_row_ref, next_column_ref,
+    row_ref, column_ref, *scratch,
+):
+    split_cells(tile_ref, bed_ref, 1, row_ref, column_ref)
+    split_cells(tile_ref, bed_ref, 2, next_row_ref, next_column_ref)
     mass, frac = decode(state_ref[pl.ds(3, 2 * NB, stride=4), :])
-    dep_ref[...] = mass * (1.0 - frac) * frac
-    out_ref[...] = before_ref[...] + histogram(tile_ref, bed_ref, dep_ref, 1)
+    dep = mass * (1.0 - frac) * frac
+    out_ref[...] = before_ref[...] + histogram(row_ref, column_ref, dep, *scratch)
 
 
 def bed_third_kernel(
-    tile_ref, bed_ref, state_ref, before_ref, mass_ref, own_ref, peer_ref, dep_ref
+    row_ref, column_ref, state_ref, before_ref, mass_ref, own_ref, peer_ref, *scratch
 ):
     mass, frac = decode(state_ref[pl.ds(3, 2 * NB, stride=4), :])
     left = mass * (1.0 - frac) * (1.0 - frac)
-    dep_ref[...] = left * frac
     mass_ref[...] = left * (1.0 - frac)
-    total = before_ref[...] + histogram(tile_ref, bed_ref, dep_ref, 2)
+    total = before_ref[...] + histogram(row_ref, column_ref, left * frac, *scratch)
     total = total * (BEDC / PARTS)
     first = lax.axis_index("arch") == 0
     own_ref[...] = jnp.where(first, total[0:4], total[4:8])
@@ -267,7 +290,8 @@
     bed_type = jax.ShapeDtypeStruct((8, 128), jnp.float32)
     steps = NB // CHUNK
     span = CHUNK * WIDTH
-    dep_scratch = [pltpu.VMEM((2 * NB, 128), jnp.float32)]
+    runs = jax.ShapeDtypeStruct((2 * NB, 128), jnp.float32)
+    bed_scratch = [in_vmem(runs), in_vmem(runs), pltpu.VMEM((16, 128), jnp.float32)]
 
     outgoing = pl.pallas_call(
         first_kernel,
@@ -316,7 +340,7 @@
         in_specs=[whole(SMEM), whole(), whole(), whole()],
         out_specs=whole(),
         out_shape=bed_type,
-        scratch_shapes=dep_scratch,
+        scratch_shapes=[in_vmem(runs), in_vmem(runs)] + bed_scratch,
         compiler_params=params(),
         cost_estimate=pl.CostEstimate(flops=10**9, bytes_accessed=10**7, transcendentals=0),
         name="bed_first",
@@ -331,12 +355,12 @@
         name="relay",
     )(route_code, incoming, second)
 
-    bed = pl.pallas_call(
+    bed, row, column = pl.pallas_call(
         bed_second_kernel,
         in_specs=[whole(SMEM), whole(), whole(), whole()],
-        out_specs=whole(),
-        out_shape=bed_type,
-        scratch_shapes=dep_scratch,
+        out_specs=[whole(), whole(), whole()],
+        out_shape=[bed_type, in_vmem(runs), in_vmem(runs)],
+        scratch_shapes=[in_vmem(runs), in_vmem(runs)] + bed_scratch,
         compiler_params=params(),
         cost_estimate=pl.CostEstimate(flops=10**9, bytes_accessed=10**7, transcendentals=0),
         name="bed_second",
@@ -346,17 +370,17 @@
 
     final_mass, own, peer = pl.pallas_call(
         bed_third_kernel,
-        in_specs=[whole(SMEM), whole(), whole(), whole()],
+        in_specs=[whole()] * 4,
         out_specs=[whole(), whole(), whole()],
         out_shape=[
             jax.ShapeDtypeStruct((2 * NB, 128), jnp.float32),
             jax.ShapeDtypeStruct((4, 128), jnp.float32),
             jax.ShapeDtypeStruct((4, 128), jnp.float32),
         ],
-        scratch_shapes=dep_scratch,
+        scratch_shapes=bed_scratch,
         compiler_params=params(),
         name="bed_third",
-    )(block_tile, bed_cell, incoming.reshape(8 * NB, 128), bed)
+    )(row, column, incoming.reshape(8 * NB, 128), bed)
     other = lax.ppermute(peer, "arch", swap)
 
     final_position = pl.pallas_call(

time: 78.9 us -> 76.7 us (0.972)
  Pallas kernels: 25.5 us -> 23.7 us
    pallas_call x1, Pallas kernels: 3.77 us -> 1.56 us  [body(): pl.pallas_call(bed_third_kernel, in_specs=[whole()] * 4, out_specs=[whole...]
    pallas_call x1, Pallas kernels: 3.27 us -> 4.13 us  [body(): pl.pallas_call(bed_second_kernel, in_specs=[whole(SMEM), whole(), whole()...]
  transfers between devices with their start and end apart: 5 -> 5, of which waited for: 3 -> 3; matrix products, arithmetic and copies ran while one was open for 0% -> 0% of each run, Pallas kernels for 19% -> 20%
where the time goes in v3:
time: 76.7 us; the launch traced here: 76.5 us
  starting transfers between devices  28.2 us (37%)
  Pallas kernels  23.7 us (31%)
  waiting for transfers between devices  23.2 us (30%)
    all_to_all x2, waiting for transfers between devices, body(): incoming = lax.all_to_all(outgoing, 'dom', 0, 0, tiled=True)  21.9 us
    all_to_all x2, starting transfers between devices, body(): incoming = lax.all_to_all(outgoing, 'dom', 0, 0, tiled=True)  20.4 us
    pallas_call x1, Pallas kernels, body(): pl.pallas_call(later_kernel, grid=(steps,), in_specs=[whole(SMEM), whole(...  7.26 us
    pallas_call x1, Pallas kernels, body(): pl.pallas_call(first_kernel, grid=(steps,), in_specs=[whole(SMEM), whole(...  5.16 us
    ppermute x1, starting transfers between devices, body(): other = lax.ppermute(peer, 'arch', swap)  4.42 us
    pallas_call x1, Pallas kernels, body(): pl.pallas_call(bed_second_kernel, in_specs=[whole(SMEM), whole(), whole()...  4.13 us
    ppermute x1, starting transfers between devices, body(): peer_vel = lax.ppermute(vel, 'arch', swap)  3.33 us
    pallas_call x1, Pallas kernels, body(): pl.pallas_call(bed_first_kernel, in_specs=[whole(SMEM), whole(), whole(),...  2.83 us
  transfers between devices with their start and end apart: 5, of which 3 were waited for; matrix products, arithmetic and copies ran while one was open for 0% of the time, Pallas kernels for 20%

profile of v3, /device:TPU:1, one launch (start us, length us, event | category | flops | bytes accessed | tf_op | source)
XLA Modules:
  0.0 76.5 jit_solution(912862283829480800)
XLA Ops:
  0.6 3.3 %collective-permute-start = (bf16[3,4,2048]{2,1,0:T(4,128)(2,1)}, bf16[3,4,2048]{2,1,0:T(4,128)(2,1)S(1)}, u32[]{:S(2)}, u32[]{:S(2)}) collective-permute-start(bf16[3,4,2048]{2,1,0:T(4,128)(2,1)} %bitcast.18), channel_id=1, source_target_pairs={{0,128},{128,0},{1,129},{129,1},{2,130},{130,2},{3,131},{131,3},{4... | collective-permute-start | bytes 147464 | tf_op jit(solution)/shard_map/ppermute | solution.py:283
  4.0 0.1 collective-permute-start.1
  4.1 1.3 %collective-permute-done.1.peer_dif = bf16[4,2048]{1,0:T(4,128)(2,1)S(1)} collective-permute-done((bf16[4,2048]{1,0:T(4,128)(2,1)}, bf16[4,2048]{1,0:T(4,128)(2,1)S(1)}, u32[]{:S(2)}, u32[]{:S(2)}) %collective-permute-start.1) | collective-permute-done | bytes 16416 | tf_op jit(solution)/shard_map/ppermute | solution.py:284
  5.4 0.0 collective-permute-done.peer_vel
  5.4 5.2 %first.1 = s32[128,8,128]{2,1,0:T(8,128)} custom-call(s32[3,1,128]{2,1,0:T(1,128)} %tile_ref.7, s32[2,1,128]{2,1,0:T(1,128)} %route_ref.3, bf16[3,4,2048]{2,1,0:T(4,128)(2,1)} %bitcast.19, bf16[3,4,2048]{2,1,0:T(4,128)(2,1)S(1)} %collective-permute-done.peer_vel, bf16[4,2048]{1,0:T(4,128)(2,1)} %bitcast.22, ...), custom_call_target="tpu_custom_call" | custom-call | tf_op jit(solution)/shard_map/first/pallas_call | solution.py:296
  10.5 13.8 %all-to-all-start = ((s32[128,8,128]{2,1,0:T(8,128)}), s32[128,8,128]{2,1,0:T(8,128)S(1)}, u32[]{:S(2)}, u32[]{:S(2)}) async-start(s32[128,8,128]{2,1,0:T(8,128)} %first.1), calls=%async_computation | async-start | bytes 1048576 | tf_op jit(solution)/shard_map/all_to_all | solution.py:320
  24.3 0.0 copy-start.2
  24.3 7.3 %later.1 = (s32[128,8,128]{2,1,0:T(8,128)S(1)}, f32[128,8,128]{2,1,0:T(8,128)S(1)}) custom-call(s32[3,1,128]{2,1,0:T(1,128)} %tile_ref.7, bf16[3,4,2048]{2,1,0:T(4,128)(2,1)} %bitcast.20, bf16[3,4,2048]{2,1,0:T(4,128)(2,1)S(1)} %collective-permute-done.peer_vel, bf16[4,2048]{1,0:T(4,128)(2,1)} %bitcast.23, ...), custom_call_target="tpu_custom_call" | custom-call | flops 1000000000 | bytes 10000000 | tf_op jit(solution)/shard_map/later/pallas_call | solution.py:322
  31.6 0.0 copy-start
  31.6 0.0 copy-start.1
  31.6 0.0 copy-start.3
  31.6 0.0 copy-start.4
  31.6 11.7 %all-to-all-done.in_ref = s32[128,8,128]{2,1,0:T(8,128)S(1)} async-done(((s32[128,8,128]{2,1,0:T(8,128)}), s32[128,8,128]{2,1,0:T(8,128)S(1)}, u32[]{:S(2)}, u32[]{:S(2)}) %all-to-all-start) | async-done | bytes 524320 | tf_op jit(solution)/shard_map/all_to_all | solution.py:320
  43.3 0.0 copy-done.2
  43.3 1.7 %relay.1 = s32[128,8,128]{2,1,0:T(8,128)} custom-call(s32[2,1,128]{2,1,0:T(1,128)S(1)} %copy-done.2, s32[128,8,128]{2,1,0:T(8,128)S(1)} %all-to-all-done.in_ref, s32[128,8,128]{2,1,0:T(8,128)S(1)} %get-tuple-element.11.add_ref), custom_call_target="tpu_custom_call" | custom-call | tf_op jit(solution)/shard_map/relay/pallas_call | solution.py:349
  45.0 6.6 %all-to-all-start.1 = ((s32[128,8,128]{2,1,0:T(8,128)}), s32[128,8,128]{2,1,0:T(8,128)S(1)}, u32[]{:S(2)}, u32[]{:S(2)}) async-start(s32[128,8,128]{2,1,0:T(8,128)} %relay.1), calls=%async_computation.1 | async-start | bytes 1048576 | tf_op jit(solution)/shard_map/all_to_all | solution.py:369
  51.6 0.0 copy-done
  51.6 0.0 copy-done.1
  51.6 0.0 copy-done.3
  51.6 0.0 copy-done.4
  51.6 2.8 %bed_first.1.before_ref = f32[8,128]{1,0:T(8,128)S(1)} custom-call(s32[3,1,128]{2,1,0:T(1,128)S(1)} %copy-done.3, s32[3,32768]{1,0:T(4,128)S(1)} %copy-done.4, f32[256,128]{1,0:T(8,128)S(1)} %bitcast.15, f32[256,128]{1,0:T(8,128)S(1)} %bitcast.17), custom_call_target="tpu_custom_call" | custom-call | flops 1000000000 | bytes 10000000 | tf_op jit(solution)/shard_map/bed_first/pallas_call | solution.py:338
  54.5 4.1 %bed_second.1 = (f32[8,128]{1,0:T(8,128)S(1)}, f32[256,128]{1,0:T(8,128)S(1)}, f32[256,128]{1,0:T(8,128)S(1)}) custom-call(s32[3,1,128]{2,1,0:T(1,128)S(1)} %copy-done.3, s32[3,32768]{1,0:T(4,128)S(1)} %copy-done.4, s32[1024,128]{1,0:T(8,128)S(1)} %bitcast.13, f32[8,128]{1,0:T(8,128)S(1)} %bed_first.1.before_ref), custom_call_target="tpu_custom_call" | custom-call | flops 1000000000 | bytes 10000000 | tf_op jit(solution)/shard_map/bed_second/pallas_call | solution.py:358
  58.6 10.2 %all-to-all-done.1.in_ref = s32[128,8,128]{2,1,0:T(8,128)S(1)} async-done(((s32[128,8,128]{2,1,0:T(8,128)}), s32[128,8,128]{2,1,0:T(8,128)S(1)}, u32[]{:S(2)}, u32[]{:S(2)}) %all-to-all-start.1) | async-done | bytes 524320 | tf_op jit(solution)/shard_map/all_to_all | solution.py:369
  68.8 1.6 %bed_third.1 = (f32[256,128]{1,0:T(8,128)}, f32[4,128]{1,0:T(4,128)S(1)}, f32[4,128]{1,0:T(4,128)S(1)}) custom-call(f32[256,128]{1,0:T(8,128)S(1)} %get-tuple-element.13.row_ref, f32[256,128]{1,0:T(8,128)S(1)} %get-tuple-element.14.column_ref, s32[1024,128]{1,0:T(8,128)S(1)} %bitcast.12, f32[8,128]{1,0:T(8,128)S(1)} %get-tuple-element.15.before_ref), custom_call_target="tpu_custom_call" | custom-call | tf_op jit(solution)/shard_map/bed_third/pallas_call | solution.py:371
  70.4 4.4 %collective-permute-start.2 = (f32[4,128]{1,0:T(4,128)S(1)}, f32[4,128]{1,0:T(4,128)S(1)}, u32[]{:S(2)}, u32[]{:S(2)}) collective-permute-start(f32[4,128]{1,0:T(4,128)S(1)} %get-tuple-element.18), channel_id=1, source_target_pairs={{0,128},{128,0},{1,129},{129,1},{2,130},{130,2},{3,131},{131,3},{4... | collective-permute-start | bytes 6152 | tf_op jit(solution)/shard_map/ppermute | solution.py:384
  74.8 1.1 %finish.1 = f32[3,32768]{1,0:T(4,128)} custom-call(s32[128,8,128]{2,1,0:T(8,128)S(1)} %all-to-all-done.1.in_ref, f32[128,8,128]{2,1,0:T(8,128)S(1)} %get-tuple-element.12.add_ref), custom_call_target="tpu_custom_call" | custom-call | flops 10000000 | bytes 1000000 | tf_op jit(solution)/shard_map/finish/pallas_call | solution.py:386
  75.9 0.0 collective-permute-done.2
  75.9 0.6 add.3
Async XLA Ops:
  0.6 4.7 %collective-permute-start = (bf16[3,4,2048]{2,1,0:T(4,128)(2,1)}, bf16[3,4,2048]{2,1,0:T(4,128)(2,1)S(1)}, u32[]{:S(2)}, u32[]{:S(2)}) collective-permute-start(bf16[3,4,2048]{2,1,0:T(4,128)(2,1)} %bitcast.18), channel_id=1, source_target_pairs={{0,128},{128,0},{1,129},{129,1},{2,130},{130,2},{3,131},{131,3},{4... | collective-permute-start | bytes 147464 | tf_op jit(solution)/shard_map/ppermute | solution.py:283
  4.0 1.4 %collective-permute-start.1 = (bf16[4,2048]{1,0:T(4,128)(2,1)}, bf16[4,2048]{1,0:T(4,128)(2,1)S(1)}, u32[]{:S(2)}, u32[]{:S(2)}) collective-permute-start(bf16[4,2048]{1,0:T(4,128)(2,1)} %bitcast.21), channel_id=1, source_target_pairs={{0,128},{128,0},{1,129},{129,1},{2,130},{130,2},{3,131},{131,3},{4... | collective-permute-start | bytes 49160 | tf_op jit(solution)/shard_map/ppermute | solution.py:284
  10.5 32.8 %all-to-all-start = ((s32[128,8,128]{2,1,0:T(8,128)}), s32[128,8,128]{2,1,0:T(8,128)S(1)}, u32[]{:S(2)}, u32[]{:S(2)}) async-start(s32[128,8,128]{2,1,0:T(8,128)} %first.1), calls=%async_computation | async-start | bytes 1048576 | tf_op jit(solution)/shard_map/all_to_all | solution.py:320
  24.3 19.0 %copy-start.2 = (s32[2,1,128]{2,1,0:T(1,128)S(1)}, s32[2,1,128]{2,1,0:T(1,128)}, u32[]{:S(2)}) copy-start(s32[2,1,128]{2,1,0:T(1,128)} %route_ref.3) | copy-start | bytes 3076
  31.6 20.0 %copy-start = (f32[32768]{0:T(1024)S(1)}, f32[32768]{0:T(1024)}, u32[]{:S(2)}) copy-start(f32[32768]{0:T(1024)} %param.11) | copy-start | bytes 393220
  31.6 20.0 %copy-start.1 = (f32[32768]{0:T(1024)S(1)}, f32[32768]{0:T(1024)}, u32[]{:S(2)}) copy-start(f32[32768]{0:T(1024)} %param.12) | copy-start | bytes 393220
  31.6 20.0 %copy-start.3 = (s32[3,1,128]{2,1,0:T(1,128)S(1)}, s32[3,1,128]{2,1,0:T(1,128)}, u32[]{:S(2)}) copy-start(s32[3,1,128]{2,1,0:T(1,128)} %tile_ref.7) | copy-start | bytes 4612
  31.6 20.0 %copy-start.4 = (s32[3,32768]{1,0:T(4,128)S(1)}, s32[3,32768]{1,0:T(4,128)}, u32[]{:S(2)}) copy-start(s32[3,32768]{1,0:T(4,128)} %bed_ref.3) | copy-start | bytes 1179652
  45.0 23.8 %all-to-all-start.1 = ((s32[128,8,128]{2,1,0:T(8,128)}), s32[128,8,128]{2,1,0:T(8,128)S(1)}, u32[]{:S(2)}, u32[]{:S(2)}) async-start(s32[128,8,128]{2,1,0:T(8,128)} %relay.1), calls=%async_computation.1 | async-start | bytes 1048576 | tf_op jit(solution)/shard_map/all_to_all | solution.py:369
  70.4 5.5 %collective-permute-start.2 = (f32[4,128]{1,0:T(4,128)S(1)}, f32[4,128]{1,0:T(4,128)S(1)}, u32[]{:S(2)}, u32[]{:S(2)}) collective-permute-start(f32[4,128]{1,0:T(4,128)S(1)} %get-tuple-element.18), channel_id=1, source_target_pairs={{0,128},{128,0},{1,129},{129,1},{2,130},{130,2},{3,131},{131,3},{4... | collective-permute-start | bytes 6152 | tf_op jit(solution)/shard_map/ppermute | solution.py:384

commit v4 on v3

--- a/solution.py
+++ b/solution.py
@@ -18,7 +18,9 @@
 FIRST_UNROLL = 32
 LATER_UNROLL = 16
 
-POS_SCALE = 2.0**26
+LINES = 6
+FIRST_CODE = (16.0, 2.0**16)
+SECOND_CODE = (24.0, 43690.0)
 MASS_SCALE = 32767.0
 FRAC_SCALE = 166000.0
 
@@ -54,19 +56,46 @@
             value = 0.5 * DT * total if c < 3 else jnp.sqrt(DT * total)
             for r in range(ROWS):
                 row = value[:, 128 * r : 128 * (r + 1)]
-                tables[slot, tile, r, c : c + 1, :] = row
-                tables[slot, tile, r, c + 4 : c + 5, :] = row
+                for at in (c, c + 3) if c < 3 else (6, 7):
+                    tables[slot, tile, r, at : at + 1, :] = row
 
 
 def halves(low, high, sub):
-    return jnp.where(sub < 4, jnp.broadcast_to(low, (8, 128)), jnp.broadcast_to(high, (8, 128)))
+    of_low = (sub < 3) | (sub == 6)
+    return jnp.where(of_low, jnp.broadcast_to(low, (8, 128)), jnp.broadcast_to(high, (8, 128)))
 
 
 def stack_halves(ref, lead, start):
     low = ref[lead + (slice(None), pl.ds(start, 128))]
     high = ref[lead + (slice(None), pl.ds(start + 128, 128))]
-    gap = jnp.zeros((1, 128), jnp.float32)
-    return jnp.concatenate([low, gap, high, gap], axis=0)
+    return jnp.concatenate([low, high, jnp.zeros((2, 128), jnp.float32)], axis=0)
+
+
+def is_z(sub):
+    return (sub == 2) | (sub == 5)
+
+
+def encode(here, state, code, sub):
+    offset, scale = code
+    scales = jnp.where(is_z(sub), 2.0 * scale, scale)
+    number = (here * scales + (offset * scales + 0.5)).astype(jnp.int32)
+    upper = pltpu.roll(number, 6, 0) >> 11
+    lower = pltpu.roll(number, 7, 0) & 2047
+    word = (number << 11) | jnp.where((sub == 0) | (sub == 3), upper, lower)
+    return jnp.where(is_z(sub), state, word)
+
+
+def load_block(ref, j):
+    rows = ref[pl.ds(LINES * j, LINES), :]
+    return jnp.concatenate([rows, jnp.zeros((2, 128), jnp.int32)], axis=0)
+
+
+def decode_position(word, code, sub):
+    offset, scale = code
+    shares = word & 2047
+    z = (pltpu.roll(shares, 2, 0) << 11) | pltpu.roll(shares, 1, 0)
+    number = jnp.where(is_z(sub), z, (word >> 11) & (2**21 - 1))
+    return number.astype(jnp.float32) * jnp.where(is_z(sub), 0.5 / scale, 1.0 / scale) - offset
 
 
 def advance(tables, slot, tile, index, noise, sub):
@@ -81,9 +110,9 @@
         values = [jnp.where(odd, b, a) for a, b in zip(values[0::2], values[1::2])]
         bit *= 2
     value = values[0]
-    spread = jnp.where((sub & 3) == 3, value, 0.0)
-    spread = spread + pltpu.roll(spread, 7, 0)
-    spread = spread + pltpu.roll(spread, 6, 0)
+    spread = jnp.take_along_axis(
+        value, jnp.where(sub < 3, 6, 7), axis=0, mode="promise_in_bounds"
+    )
     return value + spread * noise
 
 
@@ -114,8 +143,7 @@
     frac_code = jnp.clip(frac_code, 0, 65535)
     code_ref[...] = mass_code * 65536 + frac_code
     sub = sublane()
-    state_row = (sub & 3) == 3
-    fall = jnp.where((sub & 3) == 2, -3.0 * DT, 0.0)
+    fall = jnp.where(is_z(sub), -3.0 * DT, 0.0)
 
     def block(j, carry):
         start = pl.multiple_of(j * WIDTH, WIDTH)
@@ -127,8 +155,8 @@
         here = here + fall * speed
         here = here + advance(tables, 0, tile_ref[0, 0, slot] // TILES, index, noise, sub)
         state = halves(code_ref[pl.ds(2 * j, 1), :], code_ref[pl.ds(2 * j + 1, 1), :], sub)
-        code = jnp.where(state_row, state, (here * POS_SCALE).astype(jnp.int32))
-        out_ref[route_ref[0, 0, slot]] = code
+        word = encode(here, state, FIRST_CODE, sub)
+        out_ref[pl.ds(LINES * route_ref[0, 0, slot], LINES), :] = word[0:LINES]
         return carry
 
     lax.fori_loop(0, CHUNK, block, 0, unroll=FIRST_UNROLL)
@@ -147,7 +175,6 @@
             fill_tables(tables, own_vel, peer_vel, own_dif, peer_dif, step - 1, step, arch)
 
     sub = sublane()
-    state_row = (sub & 3) == 3
 
     def block(j, carry):
         start = pl.multiple_of(j * WIDTH, WIDTH)
@@ -155,22 +182,23 @@
         for step in (1, 2):
             index = cells_of(cell_ref, step, start, sub)
             noise = stack_halves(noise_ref, (step,), start)
-            moved = advance(
+            out_ref = second_ref if step == 1 else third_ref
+            out_ref[j] = advance(
                 tables, step - 1, tile_ref[step, 0, slot] // TILES, index, noise, sub
             )
-            if step == 1:
-                code = (moved * POS_SCALE).astype(jnp.int32)
-                second_ref[j] = jnp.where(state_row, 0, code)
-            else:
-                third_ref[j] = moved
         return carry
 
     lax.fori_loop(0, CHUNK, block, 0, unroll=LATER_UNROLL)
 
 
 def relay_kernel(route_ref, in_ref, add_ref, out_ref):
+    sub = sublane()
+
     def block(j, carry):
-        out_ref[route_ref[1, 0, j]] = in_ref[j] + add_ref[j]
+        word = load_block(in_ref, j)
+        here = decode_position(word, FIRST_CODE, sub) + add_ref[j]
+        word = encode(here, word, SECOND_CODE, sub)
+        out_ref[pl.ds(LINES * route_ref[1, 0, j], LINES), :] = word[0:LINES]
         return carry
 
     lax.fori_loop(0, NB, block, 0, unroll=16)
@@ -243,7 +271,7 @@
 ):
     split_cells(tile_ref, bed_ref, 1, row_ref, column_ref)
     split_cells(tile_ref, bed_ref, 2, next_row_ref, next_column_ref)
-    mass, frac = decode(state_ref[pl.ds(3, 2 * NB, stride=4), :])
+    mass, frac = decode(state_ref[pl.ds(2, 2 * NB, stride=3), :])
     dep = mass * (1.0 - frac) * frac
     out_ref[...] = before_ref[...] + histogram(row_ref, column_ref, dep, *scratch)
 
@@ -251,7 +279,7 @@
 def bed_third_kernel(
     row_ref, column_ref, state_ref, before_ref, mass_ref, own_ref, peer_ref, *scratch
 ):
-    mass, frac = decode(state_ref[pl.ds(3, 2 * NB, stride=4), :])
+    mass, frac = decode(state_ref[pl.ds(2, 2 * NB, stride=3), :])
     left = mass * (1.0 - frac) * (1.0 - frac)
     mass_ref[...] = left * (1.0 - frac)
     total = before_ref[...] + histogram(row_ref, column_ref, left * frac, *scratch)
@@ -262,14 +290,21 @@
 
 
 def finish_kernel(in_ref, add_ref, out_ref):
+    sub = sublane()
+
     def block(j, carry):
         start = pl.multiple_of(j * WIDTH, WIDTH)
-        here = in_ref[j].astype(jnp.float32) * (1.0 / POS_SCALE) + add_ref[j]
+        here = decode_position(load_block(in_ref, j), SECOND_CODE, sub) + add_ref[j]
         out_ref[:, pl.ds(start, 128)] = here[0:3]
-        out_ref[:, pl.ds(start + 128, 128)] = here[4:7]
+        out_ref[:, pl.ds(start + 128, 128)] = here[3:6]
         return carry
 
     lax.fori_loop(0, NB, block, 0, unroll=16)
+
+
+def exchange(outgoing):
+    blocks = outgoing.reshape(NB, 1, LINES * 128)
+    return lax.all_to_all(blocks, "dom", 0, 0, tiled=True).reshape(LINES * NB, 128)
 
 
 def body(
@@ -285,7 +320,7 @@
     mass = particle_mass.reshape(2 * NB, 128)
     settle = settling.reshape(2 * NB, 128)
 
-    state_type = jax.ShapeDtypeStruct((NB, 8, 128), jnp.int32)
+    state_type = jax.ShapeDtypeStruct((LINES * NB, 128), jnp.int32)
     move_type = jax.ShapeDtypeStruct((NB, 8, 128), jnp.float32)
     bed_type = jax.ShapeDtypeStruct((8, 128), jnp.float32)
     steps = NB // CHUNK
@@ -304,7 +339,7 @@
             pl.BlockSpec((1, 3, span), lambda i: (0, 0, i)),
             pl.BlockSpec((3, span), lambda i: (0, i)),
         ],
-        out_specs=pl.BlockSpec((NB, 8, 128), lambda i: (0, 0, 0)),
+        out_specs=pl.BlockSpec((LINES * NB, 128), lambda i: (0, 0)),
         out_shape=state_type,
         scratch_shapes=[
             pltpu.VMEM((1, 2, ROWS, 8, 128), jnp.float32),
@@ -317,7 +352,7 @@
         *in_hbm(position, mass, settle, walk_noise, cell_index),
     )
 
-    incoming = lax.all_to_all(outgoing, "dom", 0, 0, tiled=True)
+    incoming = exchange(outgoing)
 
     second, third = pl.pallas_call(
         later_kernel,
@@ -328,7 +363,7 @@
             pl.BlockSpec((3, span), lambda i: (0, i)),
         ],
         out_specs=[pl.BlockSpec((CHUNK, 8, 128), lambda i: (i, 0, 0))] * 2,
-        out_shape=[in_vmem(state_type), in_vmem(move_type)],
+        out_shape=[in_vmem(move_type), in_vmem(move_type)],
         scratch_shapes=[pltpu.VMEM((2, 2, ROWS, 8, 128), jnp.float32)],
         compiler_params=params(),
         cost_estimate=pl.CostEstimate(flops=10**9, bytes_accessed=10**7, transcendentals=0),
@@ -364,9 +399,9 @@
         compiler_params=params(),
         cost_estimate=pl.CostEstimate(flops=10**9, bytes_accessed=10**7, transcendentals=0),
         name="bed_second",
-    )(block_tile, bed_cell, incoming.reshape(8 * NB, 128), bed)
-
-    incoming = lax.all_to_all(outgoing, "dom", 0, 0, tiled=True)
+    )(block_tile, bed_cell, incoming, bed)
+
+    incoming = exchange(outgoing)
 
     final_mass, own, peer = pl.pallas_call(
         bed_third_kernel,
@@ -380,7 +415,7 @@
         scratch_shapes=bed_scratch,
         compiler_params=params(),
         name="bed_third",
-    )(row, column, incoming.reshape(8 * NB, 128), bed)
+    )(row, column, incoming, bed)
     other = lax.ppermute(peer, "arch", swap)
 
     final_position = pl.pallas_call(

time: 76.7 us -> 71.4 us (0.931)
  waiting for transfers between devices: 23.2 us -> 18.2 us
    all_to_all x2, waiting for transfers between devices: 21.9 us -> 16.9 us  [exchange(): lax.all_to_all(blocks, 'dom', 0, 0, tiled=True).reshape(LINES * NB, 128)]
  transfers between devices with their start and end apart: 5 -> 5, of which waited for: 3 -> 3; matrix products, arithmetic and copies ran while one was open for 0% -> 0% of each run, Pallas kernels for 20% -> 22%
where the time goes in v4:
time: 71.4 us; the launch traced here: 71.1 us
  starting transfers between devices  27.7 us (39%)
  Pallas kernels  23.9 us (33%)
  waiting for transfers between devices  18.2 us (25%)
  between operations  0.73 us (1%)
    all_to_all x2, starting transfers between devices, exchange(): lax.all_to_all(blocks, 'dom', 0, 0, tiled=True).reshape(LINES * NB, 128)  20 us
    all_to_all x2, waiting for transfers between devices, exchange(): lax.all_to_all(blocks, 'dom', 0, 0, tiled=True).reshape(LINES * NB, 128)  16.9 us
    pallas_call x1, Pallas kernels, body(): pl.pallas_call(later_kernel, grid=(steps,), in_specs=[whole(SMEM), whole(...  7.23 us
    pallas_call x1, Pallas kernels, body(): pl.pallas_call(first_kernel, grid=(steps,), in_specs=[whole(SMEM), whole(...  5.13 us
    ppermute x1, starting transfers between devices, body(): other = lax.ppermute(peer, 'arch', swap)  4.28 us
    pallas_call x1, Pallas kernels, body(): pl.pallas_call(bed_second_kernel, in_specs=[whole(SMEM), whole(), whole()...  4.13 us
    ppermute x1, starting transfers between devices, body(): peer_vel = lax.ppermute(vel, 'arch', swap)  3.33 us
    pallas_call x1, Pallas kernels, body(): pl.pallas_call(bed_first_kernel, in_specs=[whole(SMEM), whole(), whole(),...  2.83 us
  transfers between devices with their start and end apart: 5, of which 3 were waited for; matrix products, arithmetic and copies ran while one was open for 0% of the time, Pallas kernels for 22%

profile of v4, /device:TPU:1, one launch (start us, length us, event | category | flops | bytes accessed | tf_op | source)
XLA Modules:
  0.0 71.1 jit_solution(16881718599525614160)
XLA Ops:
  0.6 3.3 %collective-permute-start = (bf16[3,4,2048]{2,1,0:T(4,128)(2,1)}, bf16[3,4,2048]{2,1,0:T(4,128)(2,1)S(1)}, u32[]{:S(2)}, u32[]{:S(2)}) collective-permute-start(bf16[3,4,2048]{2,1,0:T(4,128)(2,1)} %bitcast.22), channel_id=1, source_target_pairs={{0,128},{128,0},{1,129},{129,1},{2,130},{130,2},{3,131},{131,3},{4... | collective-permute-start | bytes 147464 | tf_op jit(solution)/shard_map/ppermute | solution.py:318
  4.0 0.1 collective-permute-start.1
  4.1 1.3 %collective-permute-done.1.peer_dif = bf16[4,2048]{1,0:T(4,128)(2,1)S(1)} collective-permute-done((bf16[4,2048]{1,0:T(4,128)(2,1)}, bf16[4,2048]{1,0:T(4,128)(2,1)S(1)}, u32[]{:S(2)}, u32[]{:S(2)}) %collective-permute-start.1) | collective-permute-done | bytes 16416 | tf_op jit(solution)/shard_map/ppermute | solution.py:319
  5.4 0.0 collective-permute-done.peer_vel
  5.4 5.1 %first.1 = s32[768,128]{1,0:T(8,128)} custom-call(s32[3,1,128]{2,1,0:T(1,128)} %tile_ref.7, s32[2,1,128]{2,1,0:T(1,128)} %route_ref.3, bf16[3,4,2048]{2,1,0:T(4,128)(2,1)} %bitcast.23, bf16[3,4,2048]{2,1,0:T(4,128)(2,1)S(1)} %collective-permute-done.peer_vel, bf16[4,2048]{1,0:T(4,128)(2,1)} %bitcast.26, bf16[4,2048]{1,0:T(4,128)(2,1)S(1)} %collective-permute-done.1.peer_dif, ...), custom_call_target="tpu_custom_call" | custom-call | tf_op jit(solution)/shard_map/first/pallas_call | solution.py:331
  10.5 13.8 %all-to-all-start = ((s32[128,1,768]{2,1,0:T(1,128)}), s32[128,1,768]{2,1,0:T(1,128)S(1)}, u32[]{:S(2)}, u32[]{:S(2)}) async-start(s32[128,1,768]{2,1,0:T(1,128)} %bitcast.8), calls=%async_computation | async-start | bytes 786432 | tf_op jit(solution)/shard_map/all_to_all | solution.py:307
  24.3 0.0 copy-start.2
  24.3 7.2 %later.1 = (f32[128,8,128]{2,1,0:T(8,128)S(1)}, f32[128,8,128]{2,1,0:T(8,128)S(1)}) custom-call(s32[3,1,128]{2,1,0:T(1,128)} %tile_ref.7, bf16[3,4,2048]{2,1,0:T(4,128)(2,1)} %bitcast.24, bf16[3,4,2048]{2,1,0:T(4,128)(2,1)S(1)} %collective-permute-done.peer_vel, bf16[4,2048]{1,0:T(4,128)(2,1)} %bitcast.27, ...), custom_call_target="tpu_custom_call" | custom-call | flops 1000000000 | bytes 10000000 | tf_op jit(solution)/shard_map/later/pallas_call | solution.py:357
  31.5 0.0 copy-start
  31.5 0.0 copy-start.1
  31.5 0.0 copy-start.3
  31.6 0.0 copy-start.4
  31.6 9.3 %all-to-all-done = s32[128,1,768]{2,1,0:T(1,128)S(1)} async-done(((s32[128,1,768]{2,1,0:T(1,128)}), s32[128,1,768]{2,1,0:T(1,128)S(1)}, u32[]{:S(2)}, u32[]{:S(2)}) %all-to-all-start) | async-done | bytes 393248 | tf_op jit(solution)/shard_map/all_to_all | solution.py:307
  40.9 0.0 copy-done.2
  40.9 1.8 %relay.1 = s32[768,128]{1,0:T(8,128)} custom-call(s32[2,1,128]{2,1,0:T(1,128)S(1)} %copy-done.2, s32[768,128]{1,0:T(8,128)S(1)} %bitcast.16, f32[128,8,128]{2,1,0:T(8,128)S(1)} %get-tuple-element.11.add_ref), custom_call_target="tpu_custom_call" | custom-call | tf_op jit(solution)/shard_map/relay/pallas_call | solution.py:384
  42.7 6.2 %all-to-all-start.1 = ((s32[128,1,768]{2,1,0:T(1,128)}), s32[128,1,768]{2,1,0:T(1,128)S(1)}, u32[]{:S(2)}, u32[]{:S(2)}) async-start(s32[128,1,768]{2,1,0:T(1,128)} %bitcast.10), calls=%async_computation.1 | async-start | bytes 786432 | tf_op jit(solution)/shard_map/all_to_all | solution.py:307
  48.9 0.0 copy-done
  48.9 0.0 copy-done.1
  48.9 0.0 copy-done.3
  48.9 0.0 copy-done.4
  48.9 2.8 %bed_first.1.before_ref = f32[8,128]{1,0:T(8,128)S(1)} custom-call(s32[3,1,128]{2,1,0:T(1,128)S(1)} %copy-done.3, s32[3,32768]{1,0:T(4,128)S(1)} %copy-done.4, f32[256,128]{1,0:T(8,128)S(1)} %bitcast.19, f32[256,128]{1,0:T(8,128)S(1)} %bitcast.21), custom_call_target="tpu_custom_call" | custom-call | flops 1000000000 | bytes 10000000 | tf_op jit(solution)/shard_map/bed_first/pallas_call | solution.py:373
  51.7 4.1 %bed_second.1 = (f32[8,128]{1,0:T(8,128)S(1)}, f32[256,128]{1,0:T(8,128)S(1)}, f32[256,128]{1,0:T(8,128)S(1)}) custom-call(s32[3,1,128]{2,1,0:T(1,128)S(1)} %copy-done.3, s32[3,32768]{1,0:T(4,128)S(1)} %copy-done.4, s32[768,128]{1,0:T(8,128)S(1)} %bitcast.17, f32[8,128]{1,0:T(8,128)S(1)} %bed_first.1.before_ref), custom_call_target="tpu_custom_call" | custom-call | flops 1000000000 | bytes 10000000 | tf_op jit(solution)/shard_map/bed_second/pallas_call | solution.py:393
  55.9 7.6 %all-to-all-done.1 = s32[128,1,768]{2,1,0:T(1,128)S(1)} async-done(((s32[128,1,768]{2,1,0:T(1,128)}), s32[128,1,768]{2,1,0:T(1,128)S(1)}, u32[]{:S(2)}, u32[]{:S(2)}) %all-to-all-start.1) | async-done | bytes 393248 | tf_op jit(solution)/shard_map/all_to_all | solution.py:307
  63.5 1.6 %bed_third.1 = (f32[256,128]{1,0:T(8,128)}, f32[4,128]{1,0:T(4,128)S(1)}, f32[4,128]{1,0:T(4,128)S(1)}) custom-call(f32[256,128]{1,0:T(8,128)S(1)} %get-tuple-element.13.row_ref, f32[256,128]{1,0:T(8,128)S(1)} %get-tuple-element.14.column_ref, s32[768,128]{1,0:T(8,128)S(1)} %bitcast.14, f32[8,128]{1,0:T(8,128)S(1)} %get-tuple-element.15.before_ref), custom_call_target="tpu_custom_call" | custom-call | tf_op jit(solution)/shard_map/bed_third/pallas_call | solution.py:406
  65.0 4.3 %collective-permute-start.2 = (f32[4,128]{1,0:T(4,128)S(1)}, f32[4,128]{1,0:T(4,128)S(1)}, u32[]{:S(2)}, u32[]{:S(2)}) collective-permute-start(f32[4,128]{1,0:T(4,128)S(1)} %get-tuple-element.18), channel_id=1, source_target_pairs={{0,128},{128,0},{1,129},{129,1},{2,130},{130,2},{3,131},{131,3},{4... | collective-permute-start | bytes 6152 | tf_op jit(solution)/shard_map/ppermute | solution.py:419
  69.3 1.2 %finish.1 = f32[3,32768]{1,0:T(4,128)} custom-call(s32[768,128]{1,0:T(8,128)S(1)} %bitcast.15, f32[128,8,128]{2,1,0:T(8,128)S(1)} %get-tuple-element.12.add_ref), custom_call_target="tpu_custom_call" | custom-call | flops 10000000 | bytes 1000000 | tf_op jit(solution)/shard_map/finish/pallas_call | solution.py:421
  70.5 0.0 collective-permute-done.2
  70.5 0.6 add.3
Async XLA Ops:
  0.6 4.7 %collective-permute-start = (bf16[3,4,2048]{2,1,0:T(4,128)(2,1)}, bf16[3,4,2048]{2,1,0:T(4,128)(2,1)S(1)}, u32[]{:S(2)}, u32[]{:S(2)}) collective-permute-start(bf16[3,4,2048]{2,1,0:T(4,128)(2,1)} %bitcast.22), channel_id=1, source_target_pairs={{0,128},{128,0},{1,129},{129,1},{2,130},{130,2},{3,131},{131,3},{4... | collective-permute-start | bytes 147464 | tf_op jit(solution)/shard_map/ppermute | solution.py:318
  4.0 1.4 %collective-permute-start.1 = (bf16[4,2048]{1,0:T(4,128)(2,1)}, bf16[4,2048]{1,0:T(4,128)(2,1)S(1)}, u32[]{:S(2)}, u32[]{:S(2)}) collective-permute-start(bf16[4,2048]{1,0:T(4,128)(2,1)} %bitcast.25), channel_id=1, source_target_pairs={{0,128},{128,0},{1,129},{129,1},{2,130},{130,2},{3,131},{131,3},{4... | collective-permute-start | bytes 49160 | tf_op jit(solution)/shard_map/ppermute | solution.py:319
  10.5 30.4 %all-to-all-start = ((s32[128,1,768]{2,1,0:T(1,128)}), s32[128,1,768]{2,1,0:T(1,128)S(1)}, u32[]{:S(2)}, u32[]{:S(2)}) async-start(s32[128,1,768]{2,1,0:T(1,128)} %bitcast.8), calls=%async_computation | async-start | bytes 786432 | tf_op jit(solution)/shard_map/all_to_all | solution.py:307
  24.3 16.6 %copy-start.2 = (s32[2,1,128]{2,1,0:T(1,128)S(1)}, s32[2,1,128]{2,1,0:T(1,128)}, u32[]{:S(2)}) copy-start(s32[2,1,128]{2,1,0:T(1,128)} %route_ref.3) | copy-start | bytes 3076
  31.5 17.4 %copy-start = (f32[32768]{0:T(1024)S(1)}, f32[32768]{0:T(1024)}, u32[]{:S(2)}) copy-start(f32[32768]{0:T(1024)} %param.11) | copy-start | bytes 393220
  31.5 17.4 %copy-start.1 = (f32[32768]{0:T(1024)S(1)}, f32[32768]{0:T(1024)}, u32[]{:S(2)}) copy-start(f32[32768]{0:T(1024)} %param.12) | copy-start | bytes 393220
  31.5 17.4 %copy-start.3 = (s32[3,1,128]{2,1,0:T(1,128)S(1)}, s32[3,1,128]{2,1,0:T(1,128)}, u32[]{:S(2)}) copy-start(s32[3,1,128]{2,1,0:T(1,128)} %tile_ref.7) | copy-start | bytes 4612
  31.6 17.4 %copy-start.4 = (s32[3,32768]{1,0:T(4,128)S(1)}, s32[3,32768]{1,0:T(4,128)}, u32[]{:S(2)}) copy-start(s32[3,32768]{1,0:T(4,128)} %bed_ref.3) | copy-start | bytes 1179652
  42.7 20.8 %all-to-all-start.1 = ((s32[128,1,768]{2,1,0:T(1,128)}), s32[128,1,768]{2,1,0:T(1,128)S(1)}, u32[]{:S(2)}, u32[]{:S(2)}) async-start(s32[128,1,768]{2,1,0:T(1,128)} %bitcast.10), calls=%async_computation.1 | async-start | bytes 786432 | tf_op jit(solution)/shard_map/all_to_all | solution.py:307
  65.0 5.5 %collective-permute-start.2 = (f32[4,128]{1,0:T(4,128)S(1)}, f32[4,128]{1,0:T(4,128)S(1)}, u32[]{:S(2)}, u32[]{:S(2)}) collective-permute-start(f32[4,128]{1,0:T(4,128)S(1)} %get-tuple-element.18), channel_id=1, source_target_pairs={{0,128},{128,0},{1,129},{129,1},{2,130},{130,2},{3,131},{131,3},{4... | collective-permute-start | bytes 6152 | tf_op jit(solution)/shard_map/ppermute | solution.py:419

commit v5 on v4

--- a/solution.py
+++ b/solution.py
@@ -13,9 +13,9 @@
 BEDC = 512
 TILES = 128
 DT = 0.5
-CHUNK = 64
+CHUNK = 32
 GROUP = 32
-FIRST_UNROLL = 32
+SPAN = 64
 LATER_UNROLL = 16
 
 LINES = 6
@@ -48,16 +48,15 @@
     return lax.broadcasted_iota(jnp.int32, (8, 128), 0)
 
 
-def fill_tables(tables, own_vel, peer_vel, own_dif, peer_dif, slot, step, arch):
-    for vel, dif, tile in ((own_vel, own_dif, arch), (peer_vel, peer_dif, 1 - arch)):
-        for c in range(4):
-            v = (vel[c] if c < 3 else dif[...]).astype(jnp.float32)
-            total = v[step : step + 1] + v[step + 1 : step + 2]
-            value = 0.5 * DT * total if c < 3 else jnp.sqrt(DT * total)
-            for r in range(ROWS):
-                row = value[:, 128 * r : 128 * (r + 1)]
-                for at in (c, c + 3) if c < 3 else (6, 7):
-                    tables[slot, tile, r, at : at + 1, :] = row
+def fill_table(table, vel, dif, step):
+    for c in range(4):
+        v = (vel[c] if c < 3 else dif[...]).astype(jnp.float32)
+        total = v[step : step + 1] + v[step + 1 : step + 2]
+        value = 0.5 * DT * total if c < 3 else jnp.sqrt(DT * total)
+        for r in range(ROWS):
+            row = value[:, 128 * r : 128 * (r + 1)]
+            for at in (c, c + 3) if c < 3 else (6, 7):
+                table[r, at : at + 1, :] = row
 
 
 def halves(low, high, sub):
@@ -126,59 +125,104 @@
     return 1.0 - jnp.exp(-DT * settling)
 
 
-def first_kernel(
-    tile_ref, route_ref, own_vel, peer_vel, own_dif, peer_dif,
-    pos_ref, mass_ref, settle_ref, noise_ref, cell_ref, out_ref, tables, code_ref,
-):
-    arch = lax.axis_index("arch")
-    part = pl.program_id(0)
-
-    @pl.when(part == 0)
-    def _():
-        fill_tables(tables, own_vel, peer_vel, own_dif, peer_dif, 0, 0, arch)
-
+def invert(route_ref, step, source_ref):
+    def one(j, carry):
+        source_ref[0, route_ref[step, 0, j]] = j
+        return carry
+
+    lax.fori_loop(0, NB, one, 0, unroll=16)
+
+
+def load_kernel(
+    route_in, tile_in, vel_in, dif_in, pos_in, mass_in, settle_in, noise_in, cell_in,
+    pos_out, settle_out, noise_out, cell_out, code_ref, table_ref, tile_out, source_ref,
+    mass_ref, vel_ref, dif_ref, route_ref, sems,
+):
+    pairs = [
+        (route_in, route_ref), (tile_in, tile_out), (mass_in, mass_ref), (settle_in, settle_out),
+        (vel_in, vel_ref), (dif_in, dif_ref), (cell_in, cell_out), (pos_in, pos_out),
+        (noise_in.at[0], noise_out),
+    ]
+    copies = [pltpu.make_async_copy(a, b, sems.at[i]) for i, (a, b) in enumerate(pairs)]
+    for copy in copies:
+        copy.start()
+    for copy in copies[2:4]:
+        copy.wait()
     mass_code = (mass_ref[...] * MASS_SCALE + 0.5).astype(jnp.int32)
     mass_code = jnp.clip(mass_code, 0, 65535) - 32768
-    frac_code = (fraction(settle_ref[...]) * FRAC_SCALE + 0.5).astype(jnp.int32)
+    frac_code = (fraction(settle_out[...]) * FRAC_SCALE + 0.5).astype(jnp.int32)
     frac_code = jnp.clip(frac_code, 0, 65535)
     code_ref[...] = mass_code * 65536 + frac_code
+    for copy in copies[4:6]:
+        copy.wait()
+    fill_table(table_ref, vel_ref, dif_ref, 0)
+    copies[0].wait()
+    invert(route_ref, 0, source_ref)
+    for copy in copies[1:2] + copies[6:]:
+        copy.wait()
+
+
+def send_chunks(block, rows_ref, out_ref, sems):
+    span = LINES * CHUNK
+    copies = []
+    for part in range(NB // CHUNK):
+
+        def one(k, carry, part=part):
+            rows_ref[pl.ds(part * span + LINES * k, LINES), :] = block(part * CHUNK + k)
+            return carry
+
+        lax.fori_loop(0, CHUNK, one, 0, unroll=CHUNK)
+        rows = pl.ds(part * span, span)
+        copies.append(pltpu.make_async_copy(rows_ref.at[rows], out_ref.at[rows], sems.at[part]))
+        copies[-1].start()
+    for copy in copies:
+        copy.wait()
+
+
+def first_kernel(
+    tile_ref, source_ref, peer_vel, peer_dif,
+    pos_ref, settle_ref, noise_ref, cell_ref, code_ref, table_ref, out_ref, tables, rows_ref, sems,
+):
+    arch = lax.axis_index("arch")
+    tables[0, arch] = table_ref[...]
+    fill_table(tables.at[0, 1 - arch], peer_vel, peer_dif, 0)
     sub = sublane()
     fall = jnp.where(is_z(sub), -3.0 * DT, 0.0)
 
-    def block(j, carry):
+    def block(place):
+        j = source_ref[0, place]
         start = pl.multiple_of(j * WIDTH, WIDTH)
-        slot = part * CHUNK + j
         index = cells_of(cell_ref, 0, start, sub)
-        noise = stack_halves(noise_ref, (0,), start)
+        noise = stack_halves(noise_ref, (), start)
         here = stack_halves(pos_ref, (), start)
         speed = halves(settle_ref[pl.ds(2 * j, 1), :], settle_ref[pl.ds(2 * j + 1, 1), :], sub)
         here = here + fall * speed
-        here = here + advance(tables, 0, tile_ref[0, 0, slot] // TILES, index, noise, sub)
+        here = here + advance(tables, 0, tile_ref[0, 0, j] // TILES, index, noise, sub)
         state = halves(code_ref[pl.ds(2 * j, 1), :], code_ref[pl.ds(2 * j + 1, 1), :], sub)
-        word = encode(here, state, FIRST_CODE, sub)
-        out_ref[pl.ds(LINES * route_ref[0, 0, slot], LINES), :] = word[0:LINES]
-        return carry
-
-    lax.fori_loop(0, CHUNK, block, 0, unroll=FIRST_UNROLL)
+        return encode(here, state, FIRST_CODE, sub)[0:LINES]
+
+    send_chunks(block, rows_ref, out_ref, sems)
 
 
 def later_kernel(
-    tile_ref, own_vel, peer_vel, own_dif, peer_dif, noise_ref, cell_ref,
-    second_ref, third_ref, tables,
+    tile_ref, route_ref, own_vel, peer_vel, own_dif, peer_dif, noise_ref, cell_ref,
+    second_ref, third_ref, source_ref, tables,
 ):
     arch = lax.axis_index("arch")
     part = pl.program_id(0)
 
     @pl.when(part == 0)
     def _():
+        invert(route_ref, 1, source_ref)
         for step in (1, 2):
-            fill_tables(tables, own_vel, peer_vel, own_dif, peer_dif, step - 1, step, arch)
+            fill_table(tables.at[step - 1, arch], own_vel, own_dif, step)
+            fill_table(tables.at[step - 1, 1 - arch], peer_vel, peer_dif, step)
 
     sub = sublane()
 
     def block(j, carry):
         start = pl.multiple_of(j * WIDTH, WIDTH)
-        slot = part * CHUNK + j
+        slot = part * SPAN + j
         for step in (1, 2):
             index = cells_of(cell_ref, step, start, sub)
             noise = stack_halves(noise_ref, (step,), start)
@@ -188,20 +232,19 @@
             )
         return carry
 
-    lax.fori_loop(0, CHUNK, block, 0, unroll=LATER_UNROLL)
-
-
-def relay_kernel(route_ref, in_ref, add_ref, out_ref):
+    lax.fori_loop(0, SPAN, block, 0, unroll=LATER_UNROLL)
+
+
+def relay_kernel(source_ref, in_ref, add_ref, out_ref, rows_ref, sems):
     sub = sublane()
 
-    def block(j, carry):
+    def block(place):
+        j = source_ref[0, place]
         word = load_block(in_ref, j)
         here = decode_position(word, FIRST_CODE, sub) + add_ref[j]
-        word = encode(here, word, SECOND_CODE, sub)
-        out_ref[pl.ds(LINES * route_ref[1, 0, j], LINES), :] = word[0:LINES]
-        return carry
-
-    lax.fori_loop(0, NB, block, 0, unroll=16)
+        return encode(here, word, SECOND_CODE, sub)[0:LINES]
+
+    send_chunks(block, rows_ref, out_ref, sems)
 
 
 def decode(code):
@@ -323,52 +366,67 @@
     state_type = jax.ShapeDtypeStruct((LINES * NB, 128), jnp.int32)
     move_type = jax.ShapeDtypeStruct((NB, 8, 128), jnp.float32)
     bed_type = jax.ShapeDtypeStruct((8, 128), jnp.float32)
-    steps = NB // CHUNK
-    span = CHUNK * WIDTH
+    steps = NB // SPAN
+    span = SPAN * WIDTH
     runs = jax.ShapeDtypeStruct((2 * NB, 128), jnp.float32)
     bed_scratch = [in_vmem(runs), in_vmem(runs), pltpu.VMEM((16, 128), jnp.float32)]
 
+    *loaded, tiles, sources = pl.pallas_call(
+        load_kernel,
+        in_specs=[whole(pl.ANY)] * 9,
+        out_specs=[whole()] * 6 + [whole(SMEM)] * 2,
+        out_shape=[
+            pltpu.VMEM((3, PARTS), jnp.float32),
+            in_vmem(runs),
+            pltpu.VMEM((3, PARTS), jnp.float32),
+            pltpu.VMEM((3, PARTS), jnp.int32),
+            pltpu.VMEM((2 * NB, 128), jnp.int32),
+            pltpu.VMEM((ROWS, 8, 128), jnp.float32),
+            pltpu.SMEM(block_tile.shape, jnp.int32),
+            pltpu.SMEM((1, NB), jnp.int32),
+        ],
+        scratch_shapes=[
+            in_vmem(runs), in_vmem(vel), in_vmem(dif),
+            pltpu.SMEM(route_code.shape, jnp.int32), pltpu.SemaphoreType.DMA((9,)),
+        ],
+        compiler_params=params(),
+        cost_estimate=pl.CostEstimate(flops=10**7, bytes_accessed=4 * 10**6, transcendentals=0),
+        name="load",
+    )(
+        *in_hbm(route_code, block_tile, vel, dif),
+        *in_hbm(position, mass, settle, walk_noise, cell_index),
+    )
+
+    send_scratch = [
+        pltpu.VMEM((LINES * NB, 128), jnp.int32), pltpu.SemaphoreType.DMA((NB // CHUNK,)),
+    ]
     outgoing = pl.pallas_call(
         first_kernel,
+        in_specs=[whole(SMEM), whole(SMEM)] + [whole()] * 8,
+        out_specs=whole(pltpu.HBM),
+        out_shape=state_type,
+        scratch_shapes=[pltpu.VMEM((1, 2, ROWS, 8, 128), jnp.float32)] + send_scratch,
+        compiler_params=params(),
+        name="first",
+    )(tiles, sources, peer_vel, peer_dif, *loaded)
+
+    incoming = exchange(outgoing)
+
+    second, third, later_sources = pl.pallas_call(
+        later_kernel,
         grid=(steps,),
         in_specs=[whole(SMEM), whole(SMEM), whole(), whole(), whole(), whole()]
-        + [
-            pl.BlockSpec((3, span), lambda i: (0, i)),
-            pl.BlockSpec((2 * CHUNK, 128), lambda i: (i, 0)),
-            pl.BlockSpec((2 * CHUNK, 128), lambda i: (i, 0)),
-            pl.BlockSpec((1, 3, span), lambda i: (0, 0, i)),
-            pl.BlockSpec((3, span), lambda i: (0, i)),
-        ],
-        out_specs=pl.BlockSpec((LINES * NB, 128), lambda i: (0, 0)),
-        out_shape=state_type,
-        scratch_shapes=[
-            pltpu.VMEM((1, 2, ROWS, 8, 128), jnp.float32),
-            pltpu.VMEM((2 * CHUNK, 128), jnp.int32),
-        ],
-        compiler_params=params(),
-        name="first",
-    )(
-        *in_hbm(block_tile, route_code), *in_hbm(vel), peer_vel, *in_hbm(dif), peer_dif,
-        *in_hbm(position, mass, settle, walk_noise, cell_index),
-    )
-
-    incoming = exchange(outgoing)
-
-    second, third = pl.pallas_call(
-        later_kernel,
-        grid=(steps,),
-        in_specs=[whole(SMEM), whole(), whole(), whole(), whole()]
         + [
             pl.BlockSpec((3, 3, span), lambda i: (0, 0, i)),
             pl.BlockSpec((3, span), lambda i: (0, i)),
         ],
-        out_specs=[pl.BlockSpec((CHUNK, 8, 128), lambda i: (i, 0, 0))] * 2,
-        out_shape=[in_vmem(move_type), in_vmem(move_type)],
+        out_specs=[pl.BlockSpec((SPAN, 8, 128), lambda i: (i, 0, 0))] * 2 + [whole(SMEM)],
+        out_shape=[in_vmem(move_type), in_vmem(move_type), pltpu.SMEM((1, NB), jnp.int32)],
         scratch_shapes=[pltpu.VMEM((2, 2, ROWS, 8, 128), jnp.float32)],
         compiler_params=params(),
         cost_estimate=pl.CostEstimate(flops=10**9, bytes_accessed=10**7, transcendentals=0),
         name="later",
-    )(*in_hbm(block_tile, vel), peer_vel, *in_hbm(dif), peer_dif, *in_hbm(walk_noise, cell_index))
+    )(*in_hbm(block_tile, route_code, vel), peer_vel, *in_hbm(dif), peer_dif, *in_hbm(walk_noise, cell_index))
 
     bed = pl.pallas_call(
         bed_first_kernel,
@@ -384,11 +442,12 @@
     outgoing = pl.pallas_call(
         relay_kernel,
         in_specs=[whole(SMEM), whole(), whole()],
-        out_specs=whole(),
+        out_specs=whole(pltpu.HBM),
         out_shape=state_type,
+        scratch_shapes=send_scratch,
         compiler_params=params(),
         name="relay",
-    )(route_code, incoming, second)
+    )(later_sources, incoming, second)
 
     bed, row, column = pl.pallas_call(
         bed_second_kernel,

time: 71.4 us -> 69.4 us (0.972)
  waiting for transfers between devices: 18.2 us -> 15.8 us
    ppermute x1, waiting for transfers between devices: 1.29 us -> 0.01 us  [body(): peer_dif = lax.ppermute(dif, 'arch', swap)]
    all_to_all x2, waiting for transfers between devices: 16.9 us -> 15.8 us  [exchange(): lax.all_to_all(blocks, 'dom', 0, 0, tiled=True).reshape(LINES * NB, 128)]
    pallas_call x1 -> x2, Pallas kernels: 5.13 us -> 5.04 us  [the longest x1 3.43 us: body(): pl.pallas_call(first_kernel, in_specs=[whole(SMEM), whole(SMEM)] + [whole...]
  transfers between devices with their start and end apart: 5 -> 5, of which waited for: 3 -> 2; matrix products, arithmetic and copies ran while one was open for 0% -> 0% of each run, Pallas kernels for 22% -> 25%
where the time goes in v5:
time: 69.4 us; the launch traced here: 69.1 us
  starting transfers between devices  28.4 us (41%)
  Pallas kernels  23.5 us (34%)
  waiting for transfers between devices  15.8 us (23%)
  between operations  0.76 us (1%)
    all_to_all x2, starting transfers between devices, exchange(): lax.all_to_all(blocks, 'dom', 0, 0, tiled=True).reshape(LINES * NB, 128)  20.5 us
    all_to_all x2, waiting for transfers between devices, exchange(): lax.all_to_all(blocks, 'dom', 0, 0, tiled=True).reshape(LINES * NB, 128)  15.8 us
    pallas_call x1, Pallas kernels, body(): pl.pallas_call(later_kernel, grid=(steps,), in_specs=[whole(SMEM), whole(...  7.58 us
    ppermute x1, starting transfers between devices, body(): other = lax.ppermute(peer, 'arch', swap)  4.53 us
    pallas_call x1, Pallas kernels, body(): pl.pallas_call(bed_second_kernel, in_specs=[whole(SMEM), whole(), whole()...  4.13 us
    pallas_call x1, Pallas kernels, body(): pl.pallas_call(first_kernel, in_specs=[whole(SMEM), whole(SMEM)] + [whole...  3.43 us
    ppermute x1, starting transfers between devices, body(): peer_vel = lax.ppermute(vel, 'arch', swap)  3.33 us
    pallas_call x1, Pallas kernels, body(): pl.pallas_call(bed_first_kernel, in_specs=[whole(SMEM), whole(), whole(),...  2.83 us
  transfers between devices with their start and end apart: 5, of which 2 were waited for; matrix products, arithmetic and copies ran while one was open for 0% of the time, Pallas kernels for 25%

profile of v5, /device:TPU:1, one launch (start us, length us, event | category | flops | bytes accessed | tf_op | source)
XLA Modules:
  0.0 69.1 jit_solution(10543539219663121443)
XLA Ops:
  0.6 3.3 %collective-permute-start = (bf16[3,4,2048]{2,1,0:T(4,128)(2,1)}, bf16[3,4,2048]{2,1,0:T(4,128)(2,1)S(1)}, u32[]{:S(2)}, u32[]{:S(2)}) collective-permute-start(bf16[3,4,2048]{2,1,0:T(4,128)(2,1)} %bitcast.22), channel_id=1, source_target_pairs={{0,128},{128,0},{1,129},{129,1},{2,130},{130,2},{3,131},{131,3},{4... | collective-permute-start | bytes 147464 | tf_op jit(solution)/shard_map/ppermute | solution.py:361
  4.0 0.1 collective-permute-start.1
  4.1 1.6 %load.1 = (f32[3,32768]{1,0:T(4,128)S(1)}, f32[256,128]{1,0:T(8,128)S(1)}, f32[3,32768]{1,0:T(4,128)S(1)}, s32[3,32768]{1,0:T(4,128)S(1)}, s32[256,128]{1,0:T(8,...) custom-call(s32[2,1,128]{2,1,0:T(1,128)} %route_in.1, s32[3,1,128]{2,1,0:T(1,128)} %tile_ref.5, ...), custom_call_target="tpu_custom_call" | custom-call | flops 10000000 | bytes 4000000 | tf_op jit(solution)/shard_map/load/pallas_call | solution.py:374
  5.7 0.0 collective-permute-done.1.peer_dif
  5.7 0.0 collective-permute-done.peer_vel
  5.7 3.4 %first.1 = s32[768,128]{1,0:T(8,128)} custom-call(s32[3,1,128]{2,1,0:T(1,128)S(4)} %get-tuple-element.21.tile_ref, s32[1,128]{1,0:T(1,128)S(4)} %get-tuple-element.22.source_ref, bf16[3,4,2048]{2,1,0:T(4,128)(2,1)S(1)} %collective-permute-done.peer_vel, bf16[4,2048]{1,0:T(4,128)(2,1)S(1)} %collective-permute-done.1.peer_dif, ...), custom_call_target="tpu_custom_call" | custom-call | tf_op jit(solution)/shard_map/first/pallas_call | solution.py:403
  9.1 13.8 %all-to-all-start = ((s32[128,1,768]{2,1,0:T(1,128)}), s32[128,1,768]{2,1,0:T(1,128)S(1)}, u32[]{:S(2)}, u32[]{:S(2)}) async-start(s32[128,1,768]{2,1,0:T(1,128)} %bitcast.8), calls=%async_computation | async-start | bytes 786432 | tf_op jit(solution)/shard_map/all_to_all | solution.py:350
  22.9 7.6 %later.1 = (f32[128,8,128]{2,1,0:T(8,128)S(1)}, f32[128,8,128]{2,1,0:T(8,128)S(1)}, s32[1,128]{1,0:T(1,128)S(4)}) custom-call(s32[3,1,128]{2,1,0:T(1,128)} %tile_ref.5, s32[2,1,128]{2,1,0:T(1,128)} %route_in.1, bf16[3,4,2048]{2,1,0:T(4,128)(2,1)} %bitcast.24, bf16[3,4,2048]{2,1,0:T(4,128)(2,1)S(1)} %collective-permute-done.peer_vel, ...), custom_call_target="tpu_custom_call" | custom-call | flops 1000000000 | bytes 10000000 | tf_op jit(solution)/shard_map/later/pallas_call | solution.py:415
  30.5 0.0 copy-start
  30.5 0.0 copy-start.1
  30.6 0.0 copy-start.2
  30.6 0.0 copy-start.3
  30.6 8.7 %all-to-all-done = s32[128,1,768]{2,1,0:T(1,128)S(1)} async-done(((s32[128,1,768]{2,1,0:T(1,128)}), s32[128,1,768]{2,1,0:T(1,128)S(1)}, u32[]{:S(2)}, u32[]{:S(2)}) %all-to-all-start) | async-done | bytes 393248 | tf_op jit(solution)/shard_map/all_to_all | solution.py:350
  39.2 1.1 %relay.1 = s32[768,128]{1,0:T(8,128)} custom-call(s32[1,128]{1,0:T(1,128)S(4)} %get-tuple-element.20.source_ref, s32[768,128]{1,0:T(8,128)S(1)} %bitcast.16, f32[128,8,128]{2,1,0:T(8,128)S(1)} %get-tuple-element.29.add_ref), custom_call_target="tpu_custom_call" | custom-call | tf_op jit(solution)/shard_map/relay/pallas_call | solution.py:442
  40.3 6.7 %all-to-all-start.1 = ((s32[128,1,768]{2,1,0:T(1,128)}), s32[128,1,768]{2,1,0:T(1,128)S(1)}, u32[]{:S(2)}, u32[]{:S(2)}) async-start(s32[128,1,768]{2,1,0:T(1,128)} %bitcast.10), calls=%async_computation.1 | async-start | bytes 786432 | tf_op jit(solution)/shard_map/all_to_all | solution.py:350
  47.0 0.0 copy-done
  47.0 0.0 copy-done.1
  47.0 0.0 copy-done.2
  47.0 0.0 copy-done.3
  47.1 2.8 %bed_first.1.before_ref = f32[8,128]{1,0:T(8,128)S(1)} custom-call(s32[3,1,128]{2,1,0:T(1,128)S(1)} %copy-done.2, s32[3,32768]{1,0:T(4,128)S(1)} %copy-done.3, f32[256,128]{1,0:T(8,128)S(1)} %bitcast.19, f32[256,128]{1,0:T(8,128)S(1)} %bitcast.21), custom_call_target="tpu_custom_call" | custom-call | flops 1000000000 | bytes 10000000 | tf_op jit(solution)/shard_map/bed_first/pallas_call | solution.py:431
  49.9 4.1 %bed_second.1 = (f32[8,128]{1,0:T(8,128)S(1)}, f32[256,128]{1,0:T(8,128)S(1)}, f32[256,128]{1,0:T(8,128)S(1)}) custom-call(s32[3,1,128]{2,1,0:T(1,128)S(1)} %copy-done.2, s32[3,32768]{1,0:T(4,128)S(1)} %copy-done.3, s32[768,128]{1,0:T(8,128)S(1)} %bitcast.17, f32[8,128]{1,0:T(8,128)S(1)} %bed_first.1.before_ref), custom_call_target="tpu_custom_call" | custom-call | flops 1000000000 | bytes 10000000 | tf_op jit(solution)/shard_map/bed_second/pallas_call | solution.py:452
  54.0 7.2 %all-to-all-done.1 = s32[128,1,768]{2,1,0:T(1,128)S(1)} async-done(((s32[128,1,768]{2,1,0:T(1,128)}), s32[128,1,768]{2,1,0:T(1,128)S(1)}, u32[]{:S(2)}, u32[]{:S(2)}) %all-to-all-start.1) | async-done | bytes 393248 | tf_op jit(solution)/shard_map/all_to_all | solution.py:350
  61.2 1.6 %bed_third.1 = (f32[256,128]{1,0:T(8,128)}, f32[4,128]{1,0:T(4,128)S(1)}, f32[4,128]{1,0:T(4,128)S(1)}) custom-call(f32[256,128]{1,0:T(8,128)S(1)} %get-tuple-element.31.row_ref, f32[256,128]{1,0:T(8,128)S(1)} %get-tuple-element.32.column_ref, s32[768,128]{1,0:T(8,128)S(1)} %bitcast.14, f32[8,128]{1,0:T(8,128)S(1)} %get-tuple-element.33.before_ref), custom_call_target="tpu_custom_call" | custom-call | tf_op jit(solution)/shard_map/bed_third/pallas_call | solution.py:465
  62.8 4.5 %collective-permute-start.2 = (f32[4,128]{1,0:T(4,128)S(1)}, f32[4,128]{1,0:T(4,128)S(1)}, u32[]{:S(2)}, u32[]{:S(2)}) collective-permute-start(f32[4,128]{1,0:T(4,128)S(1)} %get-tuple-element.36), channel_id=1, source_target_pairs={{0,128},{128,0},{1,129},{129,1},{2,130},{130,2},{3,131},{131,3},{4... | collective-permute-start | bytes 6152 | tf_op jit(solution)/shard_map/ppermute | solution.py:478
  67.3 1.2 %finish.1 = f32[3,32768]{1,0:T(4,128)} custom-call(s32[768,128]{1,0:T(8,128)S(1)} %bitcast.15, f32[128,8,128]{2,1,0:T(8,128)S(1)} %get-tuple-element.30.add_ref), custom_call_target="tpu_custom_call" | custom-call | flops 10000000 | bytes 1000000 | tf_op jit(solution)/shard_map/finish/pallas_call | solution.py:480
  68.5 0.0 collective-permute-done.2
  68.5 0.6 add.3
Async XLA Ops:
  0.6 5.1 %collective-permute-start = (bf16[3,4,2048]{2,1,0:T(4,128)(2,1)}, bf16[3,4,2048]{2,1,0:T(4,128)(2,1)S(1)}, u32[]{:S(2)}, u32[]{:S(2)}) collective-permute-start(bf16[3,4,2048]{2,1,0:T(4,128)(2,1)} %bitcast.22), channel_id=1, source_target_pairs={{0,128},{128,0},{1,129},{129,1},{2,130},{130,2},{3,131},{131,3},{4... | collective-permute-start | bytes 147464 | tf_op jit(solution)/shard_map/ppermute | solution.py:361
  4.0 1.7 %collective-permute-start.1 = (bf16[4,2048]{1,0:T(4,128)(2,1)}, bf16[4,2048]{1,0:T(4,128)(2,1)S(1)}, u32[]{:S(2)}, u32[]{:S(2)}) collective-permute-start(bf16[4,2048]{1,0:T(4,128)(2,1)} %bitcast.25), channel_id=1, source_target_pairs={{0,128},{128,0},{1,129},{129,1},{2,130},{130,2},{3,131},{131,3},{4... | collective-permute-start | bytes 49160 | tf_op jit(solution)/shard_map/ppermute | solution.py:362
  9.1 30.1 %all-to-all-start = ((s32[128,1,768]{2,1,0:T(1,128)}), s32[128,1,768]{2,1,0:T(1,128)S(1)}, u32[]{:S(2)}, u32[]{:S(2)}) async-start(s32[128,1,768]{2,1,0:T(1,128)} %bitcast.8), calls=%async_computation | async-start | bytes 786432 | tf_op jit(solution)/shard_map/all_to_all | solution.py:350
  30.5 16.5 %copy-start = (f32[32768]{0:T(1024)S(1)}, f32[32768]{0:T(1024)}, u32[]{:S(2)}) copy-start(f32[32768]{0:T(1024)} %param.11) | copy-start | bytes 393220
  30.5 16.5 %copy-start.1 = (f32[32768]{0:T(1024)S(1)}, f32[32768]{0:T(1024)}, u32[]{:S(2)}) copy-start(f32[32768]{0:T(1024)} %param.12) | copy-start | bytes 393220
  30.6 16.5 %copy-start.2 = (s32[3,1,128]{2,1,0:T(1,128)S(1)}, s32[3,1,128]{2,1,0:T(1,128)}, u32[]{:S(2)}) copy-start(s32[3,1,128]{2,1,0:T(1,128)} %tile_ref.5) | copy-start | bytes 4612
  30.6 16.5 %copy-start.3 = (s32[3,32768]{1,0:T(4,128)S(1)}, s32[3,32768]{1,0:T(4,128)}, u32[]{:S(2)}) copy-start(s32[3,32768]{1,0:T(4,128)} %bed_ref.3) | copy-start | bytes 1179652
  40.3 20.8 %all-to-all-start.1 = ((s32[128,1,768]{2,1,0:T(1,128)}), s32[128,1,768]{2,1,0:T(1,128)S(1)}, u32[]{:S(2)}, u32[]{:S(2)}) async-start(s32[128,1,768]{2,1,0:T(1,128)} %bitcast.10), calls=%async_computation.1 | async-start | bytes 786432 | tf_op jit(solution)/shard_map/all_to_all | solution.py:350
  62.8 5.8 %collective-permute-start.2 = (f32[4,128]{1,0:T(4,128)S(1)}, f32[4,128]{1,0:T(4,128)S(1)}, u32[]{:S(2)}, u32[]{:S(2)}) collective-permute-start(f32[4,128]{1,0:T(4,128)S(1)} %get-tuple-element.36), channel_id=1, source_target_pairs={{0,128},{128,0},{1,129},{129,1},{2,130},{130,2},{3,131},{131,3},{4... | collective-permute-start | bytes 6152 | tf_op jit(solution)/shard_map/ppermute | solution.py:478

commit v6 on v5

--- a/solution.py
+++ b/solution.py
@@ -320,29 +320,41 @@
 
 
 def bed_third_kernel(
-    row_ref, column_ref, state_ref, before_ref, mass_ref, own_ref, peer_ref, *scratch
+    row_ref, column_ref, state_ref, before_ref, own_ref, peer_ref, *scratch
 ):
     mass, frac = decode(state_ref[pl.ds(2, 2 * NB, stride=3), :])
-    left = mass * (1.0 - frac) * (1.0 - frac)
-    mass_ref[...] = left * (1.0 - frac)
-    total = before_ref[...] + histogram(row_ref, column_ref, left * frac, *scratch)
+    dep = mass * (1.0 - frac) * (1.0 - frac) * frac
+    total = before_ref[...] + histogram(row_ref, column_ref, dep, *scratch)
     total = total * (BEDC / PARTS)
     first = lax.axis_index("arch") == 0
     own_ref[...] = jnp.where(first, total[0:4], total[4:8])
     peer_ref[...] = jnp.where(first, total[4:8], total[0:4])
 
 
-def finish_kernel(in_ref, add_ref, out_ref):
+def finish_kernel(in_ref, add_ref, out_ref, mass_out, rows_ref, mass_ref, sems):
     sub = sublane()
-
-    def block(j, carry):
-        start = pl.multiple_of(j * WIDTH, WIDTH)
-        here = decode_position(load_block(in_ref, j), SECOND_CODE, sub) + add_ref[j]
-        out_ref[:, pl.ds(start, 128)] = here[0:3]
-        out_ref[:, pl.ds(start + 128, 128)] = here[3:6]
-        return carry
-
-    lax.fori_loop(0, NB, block, 0, unroll=16)
+    mass, frac = decode(in_ref[pl.ds(2, 2 * NB, stride=3), :])
+    mass_ref[...] = mass * (1.0 - frac) * (1.0 - frac) * (1.0 - frac)
+    copies = [pltpu.make_async_copy(mass_ref, mass_out, sems.at[NB // CHUNK])]
+    copies[0].start()
+    for part in range(NB // CHUNK):
+
+        def block(k, carry, part=part):
+            j = part * CHUNK + k
+            start = pl.multiple_of(j * WIDTH, WIDTH)
+            here = decode_position(load_block(in_ref, j), SECOND_CODE, sub) + add_ref[j]
+            rows_ref[:, pl.ds(start, 128)] = here[0:3]
+            rows_ref[:, pl.ds(start + 128, 128)] = here[3:6]
+            return carry
+
+        lax.fori_loop(0, CHUNK, block, 0, unroll=16)
+        span = pl.ds(part * CHUNK * WIDTH, CHUNK * WIDTH)
+        copies.append(
+            pltpu.make_async_copy(rows_ref.at[:, span], out_ref.at[:, span], sems.at[part])
+        )
+        copies[-1].start()
+    for copy in copies:
+        copy.wait()
 
 
 def exchange(outgoing):
@@ -462,12 +474,11 @@
 
     incoming = exchange(outgoing)
 
-    final_mass, own, peer = pl.pallas_call(
+    own, peer = pl.pallas_call(
         bed_third_kernel,
         in_specs=[whole()] * 4,
-        out_specs=[whole(), whole(), whole()],
+        out_specs=[whole(), whole()],
         out_shape=[
-            jax.ShapeDtypeStruct((2 * NB, 128), jnp.float32),
             jax.ShapeDtypeStruct((4, 128), jnp.float32),
             jax.ShapeDtypeStruct((4, 128), jnp.float32),
         ],
@@ -477,11 +488,15 @@
     )(row, column, incoming, bed)
     other = lax.ppermute(peer, "arch", swap)
 
-    final_position = pl.pallas_call(
+    final_position, final_mass = pl.pallas_call(
         finish_kernel,
         in_specs=[whole(), whole()],
-        out_specs=whole(),
-        out_shape=jax.ShapeDtypeStruct((3, PARTS), jnp.float32),
+        out_specs=[whole(pltpu.HBM), whole(pltpu.HBM)],
+        out_shape=[jax.ShapeDtypeStruct((3, PARTS), jnp.float32), runs],
+        scratch_shapes=[
+            pltpu.VMEM((3, PARTS), jnp.float32), in_vmem(runs),
+            pltpu.SemaphoreType.DMA((NB // CHUNK + 1,)),
+        ],
         compiler_params=params(),
         cost_estimate=pl.CostEstimate(flops=10**7, bytes_accessed=10**6, transcendentals=0),
         name="finish",

time: 69.4 us -> 69 us (level)
  no operation moved by 1% of the time
where the time goes in v6:
time: 69 us; the launch traced here: 68.8 us
  starting transfers between devices  28.5 us (41%)
  Pallas kernels  23.1 us (33%)
  waiting for transfers between devices  15.8 us (23%)
  between operations  0.78 us (1%)
    all_to_all x2, starting transfers between devices, exchange(): lax.all_to_all(blocks, 'dom', 0, 0, tiled=True).reshape(LINES * NB, 128)  20.5 us
    all_to_all x2, waiting for transfers between devices, exchange(): lax.all_to_all(blocks, 'dom', 0, 0, tiled=True).reshape(LINES * NB, 128)  15.8 us
    pallas_call x1, Pallas kernels, body(): pl.pallas_call(later_kernel, grid=(steps,), in_specs=[whole(SMEM), whole(...  7.58 us
    ppermute x1, starting transfers between devices, body(): other = lax.ppermute(peer, 'arch', swap)  4.56 us
    pallas_call x1, Pallas kernels, body(): pl.pallas_call(bed_second_kernel, in_specs=[whole(SMEM), whole(), whole()...  4.13 us
    pallas_call x1, Pallas kernels, body(): pl.pallas_call(first_kernel, in_specs=[whole(SMEM), whole(SMEM)] + [whole...  3.43 us
    ppermute x1, starting transfers between devices, body(): peer_vel = lax.ppermute(vel, 'arch', swap)  3.33 us
    pallas_call x1, Pallas kernels, body(): pl.pallas_call(bed_first_kernel, in_specs=[whole(SMEM), whole(), whole(),...  2.83 us
  transfers between devices with their start and end apart: 5, of which 2 were waited for; matrix products, arithmetic and copies ran while one was open for 0% of the time, Pallas kernels for 25%

profile of v6, /device:TPU:1, one launch (start us, length us, event | category | flops | bytes accessed | tf_op | source)
XLA Modules:
  0.0 68.8 jit_solution(14588190578930399789)
XLA Ops:
  0.6 3.3 %collective-permute-start = (bf16[3,4,2048]{2,1,0:T(4,128)(2,1)}, bf16[3,4,2048]{2,1,0:T(4,128)(2,1)S(1)}, u32[]{:S(2)}, u32[]{:S(2)}) collective-permute-start(bf16[3,4,2048]{2,1,0:T(4,128)(2,1)} %bitcast.22), channel_id=1, source_target_pairs={{0,128},{128,0},{1,129},{129,1},{2,130},{130,2},{3,131},{131,3},{4... | collective-permute-start | bytes 147464 | tf_op jit(solution)/shard_map/ppermute | solution.py:373
  4.0 0.1 collective-permute-start.1
  4.1 1.6 %load.1 = (f32[3,32768]{1,0:T(4,128)S(1)}, f32[256,128]{1,0:T(8,128)S(1)}, f32[3,32768]{1,0:T(4,128)S(1)}, s32[3,32768]{1,0:T(4,128)S(1)}, s32[256,128]{1,0:T(8,...) custom-call(s32[2,1,128]{2,1,0:T(1,128)} %route_in.1, s32[3,1,128]{2,1,0:T(1,128)} %tile_ref.5, ...), custom_call_target="tpu_custom_call" | custom-call | flops 10000000 | bytes 4000000 | tf_op jit(solution)/shard_map/load/pallas_call | solution.py:386
  5.7 0.0 collective-permute-done.1.peer_dif
  5.7 0.0 collective-permute-done.peer_vel
  5.7 3.4 %first.1 = s32[768,128]{1,0:T(8,128)} custom-call(s32[3,1,128]{2,1,0:T(1,128)S(4)} %get-tuple-element.22.tile_ref, s32[1,128]{1,0:T(1,128)S(4)} %get-tuple-element.23.source_ref, bf16[3,4,2048]{2,1,0:T(4,128)(2,1)S(1)} %collective-permute-done.peer_vel, bf16[4,2048]{1,0:T(4,128)(2,1)S(1)} %collective-permute-done.1.peer_dif, ...), custom_call_target="tpu_custom_call" | custom-call | tf_op jit(solution)/shard_map/first/pallas_call | solution.py:415
  9.1 13.8 %all-to-all-start = ((s32[128,1,768]{2,1,0:T(1,128)}), s32[128,1,768]{2,1,0:T(1,128)S(1)}, u32[]{:S(2)}, u32[]{:S(2)}) async-start(s32[128,1,768]{2,1,0:T(1,128)} %bitcast.8), calls=%async_computation | async-start | bytes 786432 | tf_op jit(solution)/shard_map/all_to_all | solution.py:362
  22.9 7.6 %later.1 = (f32[128,8,128]{2,1,0:T(8,128)S(1)}, f32[128,8,128]{2,1,0:T(8,128)S(1)}, s32[1,128]{1,0:T(1,128)S(4)}) custom-call(s32[3,1,128]{2,1,0:T(1,128)} %tile_ref.5, s32[2,1,128]{2,1,0:T(1,128)} %route_in.1, bf16[3,4,2048]{2,1,0:T(4,128)(2,1)} %bitcast.24, bf16[3,4,2048]{2,1,0:T(4,128)(2,1)S(1)} %collective-permute-done.peer_vel, ...), custom_call_target="tpu_custom_call" | custom-call | flops 1000000000 | bytes 10000000 | tf_op jit(solution)/shard_map/later/pallas_call | solution.py:427
  30.5 0.0 copy-start
  30.5 0.0 copy-start.1
  30.6 0.0 copy-start.2
  30.6 0.0 copy-start.3
  30.6 8.7 %all-to-all-done = s32[128,1,768]{2,1,0:T(1,128)S(1)} async-done(((s32[128,1,768]{2,1,0:T(1,128)}), s32[128,1,768]{2,1,0:T(1,128)S(1)}, u32[]{:S(2)}, u32[]{:S(2)}) %all-to-all-start) | async-done | bytes 393248 | tf_op jit(solution)/shard_map/all_to_all | solution.py:362
  39.2 1.1 %relay.1 = s32[768,128]{1,0:T(8,128)} custom-call(s32[1,128]{1,0:T(1,128)S(4)} %get-tuple-element.21.source_ref, s32[768,128]{1,0:T(8,128)S(1)} %bitcast.16, f32[128,8,128]{2,1,0:T(8,128)S(1)} %get-tuple-element.30.add_ref), custom_call_target="tpu_custom_call" | custom-call | tf_op jit(solution)/shard_map/relay/pallas_call | solution.py:454
  40.3 6.7 %all-to-all-start.1 = ((s32[128,1,768]{2,1,0:T(1,128)}), s32[128,1,768]{2,1,0:T(1,128)S(1)}, u32[]{:S(2)}, u32[]{:S(2)}) async-start(s32[128,1,768]{2,1,0:T(1,128)} %bitcast.10), calls=%async_computation.1 | async-start | bytes 786432 | tf_op jit(solution)/shard_map/all_to_all | solution.py:362
  47.0 0.0 copy-done
  47.0 0.0 copy-done.1
  47.0 0.0 copy-done.2
  47.1 0.0 copy-done.3
  47.1 2.8 %bed_first.1.before_ref = f32[8,128]{1,0:T(8,128)S(1)} custom-call(s32[3,1,128]{2,1,0:T(1,128)S(1)} %copy-done.2, s32[3,32768]{1,0:T(4,128)S(1)} %copy-done.3, f32[256,128]{1,0:T(8,128)S(1)} %bitcast.19, f32[256,128]{1,0:T(8,128)S(1)} %bitcast.21), custom_call_target="tpu_custom_call" | custom-call | flops 1000000000 | bytes 10000000 | tf_op jit(solution)/shard_map/bed_first/pallas_call | solution.py:443
  49.9 4.1 %bed_second.1 = (f32[8,128]{1,0:T(8,128)S(1)}, f32[256,128]{1,0:T(8,128)S(1)}, f32[256,128]{1,0:T(8,128)S(1)}) custom-call(s32[3,1,128]{2,1,0:T(1,128)S(1)} %copy-done.2, s32[3,32768]{1,0:T(4,128)S(1)} %copy-done.3, s32[768,128]{1,0:T(8,128)S(1)} %bitcast.17, f32[8,128]{1,0:T(8,128)S(1)} %bed_first.1.before_ref), custom_call_target="tpu_custom_call" | custom-call | flops 1000000000 | bytes 10000000 | tf_op jit(solution)/shard_map/bed_second/pallas_call | solution.py:464
  54.0 7.2 %all-to-all-done.1 = s32[128,1,768]{2,1,0:T(1,128)S(1)} async-done(((s32[128,1,768]{2,1,0:T(1,128)}), s32[128,1,768]{2,1,0:T(1,128)S(1)}, u32[]{:S(2)}, u32[]{:S(2)}) %all-to-all-start.1) | async-done | bytes 393248 | tf_op jit(solution)/shard_map/all_to_all | solution.py:362
  61.2 1.3 %bed_third.1 = (f32[4,128]{1,0:T(4,128)S(1)}, f32[4,128]{1,0:T(4,128)S(1)}) custom-call(f32[256,128]{1,0:T(8,128)S(1)} %get-tuple-element.34.row_ref, f32[256,128]{1,0:T(8,128)S(1)} %get-tuple-element.35.column_ref, s32[768,128]{1,0:T(8,128)S(1)} %bitcast.14, f32[8,128]{1,0:T(8,128)S(1)} %get-tuple-element.36.before_ref), custom_call_target="tpu_custom_call" | custom-call | tf_op jit(solution)/shard_map/bed_third/pallas_call | solution.py:477
  62.5 4.6 %collective-permute-start.2 = (f32[4,128]{1,0:T(4,128)S(1)}, f32[4,128]{1,0:T(4,128)S(1)}, u32[]{:S(2)}, u32[]{:S(2)}) collective-permute-start(f32[4,128]{1,0:T(4,128)S(1)} %get-tuple-element.38), channel_id=1, source_target_pairs={{0,128},{128,0},{1,129},{129,1},{2,130},{130,2},{3,131},{131,3},{4... | collective-permute-start | bytes 6152 | tf_op jit(solution)/shard_map/ppermute | solution.py:489
  67.0 1.1 %finish.1 = (f32[3,32768]{1,0:T(4,128)}, f32[256,128]{1,0:T(8,128)}) custom-call(s32[768,128]{1,0:T(8,128)S(1)} %bitcast.15, f32[128,8,128]{2,1,0:T(8,128)S(1)} %get-tuple-element.31.add_ref), custom_call_target="tpu_custom_call" | custom-call | flops 10000000 | bytes 1000000 | tf_op jit(solution)/shard_map/finish/pallas_call | solution.py:491
  68.2 0.0 collective-permute-done.2
  68.2 0.6 add.3
Async XLA Ops:
  0.6 5.1 %collective-permute-start = (bf16[3,4,2048]{2,1,0:T(4,128)(2,1)}, bf16[3,4,2048]{2,1,0:T(4,128)(2,1)S(1)}, u32[]{:S(2)}, u32[]{:S(2)}) collective-permute-start(bf16[3,4,2048]{2,1,0:T(4,128)(2,1)} %bitcast.22), channel_id=1, source_target_pairs={{0,128},{128,0},{1,129},{129,1},{2,130},{130,2},{3,131},{131,3},{4... | collective-permute-start | bytes 147464 | tf_op jit(solution)/shard_map/ppermute | solution.py:373
  4.0 1.7 %collective-permute-start.1 = (bf16[4,2048]{1,0:T(4,128)(2,1)}, bf16[4,2048]{1,0:T(4,128)(2,1)S(1)}, u32[]{:S(2)}, u32[]{:S(2)}) collective-permute-start(bf16[4,2048]{1,0:T(4,128)(2,1)} %bitcast.25), channel_id=1, source_target_pairs={{0,128},{128,0},{1,129},{129,1},{2,130},{130,2},{3,131},{131,3},{4... | collective-permute-start | bytes 49160 | tf_op jit(solution)/shard_map/ppermute | solution.py:374
  9.1 30.1 %all-to-all-start = ((s32[128,1,768]{2,1,0:T(1,128)}), s32[128,1,768]{2,1,0:T(1,128)S(1)}, u32[]{:S(2)}, u32[]{:S(2)}) async-start(s32[128,1,768]{2,1,0:T(1,128)} %bitcast.8), calls=%async_computation | async-start | bytes 786432 | tf_op jit(solution)/shard_map/all_to_all | solution.py:362
  30.5 16.5 %copy-start = (f32[32768]{0:T(1024)S(1)}, f32[32768]{0:T(1024)}, u32[]{:S(2)}) copy-start(f32[32768]{0:T(1024)} %param.11) | copy-start | bytes 393220
  30.5 16.5 %copy-start.1 = (f32[32768]{0:T(1024)S(1)}, f32[32768]{0:T(1024)}, u32[]{:S(2)}) copy-start(f32[32768]{0:T(1024)} %param.12) | copy-start | bytes 393220
  30.6 16.5 %copy-start.2 = (s32[3,1,128]{2,1,0:T(1,128)S(1)}, s32[3,1,128]{2,1,0:T(1,128)}, u32[]{:S(2)}) copy-start(s32[3,1,128]{2,1,0:T(1,128)} %tile_ref.5) | copy-start | bytes 4612
  30.6 16.5 %copy-start.3 = (s32[3,32768]{1,0:T(4,128)S(1)}, s32[3,32768]{1,0:T(4,128)}, u32[]{:S(2)}) copy-start(s32[3,32768]{1,0:T(4,128)} %bed_ref.3) | copy-start | bytes 1179652
  40.3 20.8 %all-to-all-start.1 = ((s32[128,1,768]{2,1,0:T(1,128)}), s32[128,1,768]{2,1,0:T(1,128)S(1)}, u32[]{:S(2)}, u32[]{:S(2)}) async-start(s32[128,1,768]{2,1,0:T(1,128)} %bitcast.10), calls=%async_computation.1 | async-start | bytes 786432 | tf_op jit(solution)/shard_map/all_to_all | solution.py:362
  62.5 5.7 %collective-permute-start.2 = (f32[4,128]{1,0:T(4,128)S(1)}, f32[4,128]{1,0:T(4,128)S(1)}, u32[]{:S(2)}, u32[]{:S(2)}) collective-permute-start(f32[4,128]{1,0:T(4,128)S(1)} %get-tuple-element.38), channel_id=1, source_target_pairs={{0,128},{128,0},{1,129},{129,1},{2,130},{130,2},{3,131},{131,3},{4... | collective-permute-start | bytes 6152 | tf_op jit(solution)/shard_map/ppermute | solution.py:489

commit v7 on v6

--- a/solution.py
+++ b/solution.py
@@ -347,7 +347,7 @@
             rows_ref[:, pl.ds(start + 128, 128)] = here[3:6]
             return carry
 
-        lax.fori_loop(0, CHUNK, block, 0, unroll=16)
+        lax.fori_loop(0, CHUNK, block, 0, unroll=CHUNK)
         span = pl.ds(part * CHUNK * WIDTH, CHUNK * WIDTH)
         copies.append(
             pltpu.make_async_copy(rows_ref.at[:, span], out_ref.at[:, span], sems.at[part])

time: 69 us -> 68.9 us (level)
  no operation moved by 1% of the time
where the time goes in v7:
time: 68.9 us; the launch traced here: 68.7 us
  starting transfers between devices  28.5 us (41%)
  Pallas kernels  23 us (33%)
  waiting for transfers between devices  15.8 us (23%)
  between operations  0.78 us (1%)
    all_to_all x2, starting transfers between devices, exchange(): lax.all_to_all(blocks, 'dom', 0, 0, tiled=True).reshape(LINES * NB, 128)  20.5 us
    all_to_all x2, waiting for transfers between devices, exchange(): lax.all_to_all(blocks, 'dom', 0, 0, tiled=True).reshape(LINES * NB, 128)  15.8 us
    pallas_call x1, Pallas kernels, body(): pl.pallas_call(later_kernel, grid=(steps,), in_specs=[whole(SMEM), whole(...  7.58 us
    ppermute x1, starting transfers between devices, body(): other = lax.ppermute(peer, 'arch', swap)  4.56 us
    pallas_call x1, Pallas kernels, body(): pl.pallas_call(bed_second_kernel, in_specs=[whole(SMEM), whole(), whole()...  4.13 us
    pallas_call x1, Pallas kernels, body(): pl.pallas_call(first_kernel, in_specs=[whole(SMEM), whole(SMEM)] + [whole...  3.44 us
    ppermute x1, starting transfers between devices, body(): peer_vel = lax.ppermute(vel, 'arch', swap)  3.33 us
    pallas_call x1, Pallas kernels, body(): pl.pallas_call(bed_first_kernel, in_specs=[whole(SMEM), whole(), whole(),...  2.83 us
  transfers between devices with their start and end apart: 5, of which 2 were waited for; matrix products, arithmetic and copies ran while one was open for 0% of the time, Pallas kernels for 25%

profile of v7, /device:TPU:1, one launch (start us, length us, event | category | flops | bytes accessed | tf_op | source)
XLA Modules:
  0.0 68.7 jit_solution(10018356478557652924)
XLA Ops:
  0.6 3.3 %collective-permute-start = (bf16[3,4,2048]{2,1,0:T(4,128)(2,1)}, bf16[3,4,2048]{2,1,0:T(4,128)(2,1)S(1)}, u32[]{:S(2)}, u32[]{:S(2)}) collective-permute-start(bf16[3,4,2048]{2,1,0:T(4,128)(2,1)} %bitcast.22), channel_id=1, source_target_pairs={{0,128},{128,0},{1,129},{129,1},{2,130},{130,2},{3,131},{131,3},{4... | collective-permute-start | bytes 147464 | tf_op jit(solution)/shard_map/ppermute | solution.py:373
  4.0 0.1 collective-permute-start.1
  4.1 1.6 %load.1 = (f32[3,32768]{1,0:T(4,128)S(1)}, f32[256,128]{1,0:T(8,128)S(1)}, f32[3,32768]{1,0:T(4,128)S(1)}, s32[3,32768]{1,0:T(4,128)S(1)}, s32[256,128]{1,0:T(8,...) custom-call(s32[2,1,128]{2,1,0:T(1,128)} %route_in.1, s32[3,1,128]{2,1,0:T(1,128)} %tile_ref.5, ...), custom_call_target="tpu_custom_call" | custom-call | flops 10000000 | bytes 4000000 | tf_op jit(solution)/shard_map/load/pallas_call | solution.py:386
  5.7 0.0 collective-permute-done.1.peer_dif
  5.7 0.0 collective-permute-done.peer_vel
  5.7 3.4 %first.1 = s32[768,128]{1,0:T(8,128)} custom-call(s32[3,1,128]{2,1,0:T(1,128)S(4)} %get-tuple-element.22.tile_ref, s32[1,128]{1,0:T(1,128)S(4)} %get-tuple-element.23.source_ref, bf16[3,4,2048]{2,1,0:T(4,128)(2,1)S(1)} %collective-permute-done.peer_vel, bf16[4,2048]{1,0:T(4,128)(2,1)S(1)} %collective-permute-done.1.peer_dif, ...), custom_call_target="tpu_custom_call" | custom-call | tf_op jit(solution)/shard_map/first/pallas_call | solution.py:415
  9.1 13.8 %all-to-all-start = ((s32[128,1,768]{2,1,0:T(1,128)}), s32[128,1,768]{2,1,0:T(1,128)S(1)}, u32[]{:S(2)}, u32[]{:S(2)}) async-start(s32[128,1,768]{2,1,0:T(1,128)} %bitcast.8), calls=%async_computation | async-start | bytes 786432 | tf_op jit(solution)/shard_map/all_to_all | solution.py:362
  22.9 7.6 %later.1 = (f32[128,8,128]{2,1,0:T(8,128)S(1)}, f32[128,8,128]{2,1,0:T(8,128)S(1)}, s32[1,128]{1,0:T(1,128)S(4)}) custom-call(s32[3,1,128]{2,1,0:T(1,128)} %tile_ref.5, s32[2,1,128]{2,1,0:T(1,128)} %route_in.1, bf16[3,4,2048]{2,1,0:T(4,128)(2,1)} %bitcast.24, bf16[3,4,2048]{2,1,0:T(4,128)(2,1)S(1)} %collective-permute-done.peer_vel, ...), custom_call_target="tpu_custom_call" | custom-call | flops 1000000000 | bytes 10000000 | tf_op jit(solution)/shard_map/later/pallas_call | solution.py:427
  30.5 0.0 copy-start
  30.5 0.0 copy-start.1
  30.5 0.0 copy-start.2
  30.6 0.0 copy-start.3
  30.6 8.6 %all-to-all-done = s32[128,1,768]{2,1,0:T(1,128)S(1)} async-done(((s32[128,1,768]{2,1,0:T(1,128)}), s32[128,1,768]{2,1,0:T(1,128)S(1)}, u32[]{:S(2)}, u32[]{:S(2)}) %all-to-all-start) | async-done | bytes 393248 | tf_op jit(solution)/shard_map/all_to_all | solution.py:362
  39.2 1.1 %relay.1 = s32[768,128]{1,0:T(8,128)} custom-call(s32[1,128]{1,0:T(1,128)S(4)} %get-tuple-element.21.source_ref, s32[768,128]{1,0:T(8,128)S(1)} %bitcast.16, f32[128,8,128]{2,1,0:T(8,128)S(1)} %get-tuple-element.30.add_ref), custom_call_target="tpu_custom_call" | custom-call | tf_op jit(solution)/shard_map/relay/pallas_call | solution.py:454
  40.3 6.7 %all-to-all-start.1 = ((s32[128,1,768]{2,1,0:T(1,128)}), s32[128,1,768]{2,1,0:T(1,128)S(1)}, u32[]{:S(2)}, u32[]{:S(2)}) async-start(s32[128,1,768]{2,1,0:T(1,128)} %bitcast.10), calls=%async_computation.1 | async-start | bytes 786432 | tf_op jit(solution)/shard_map/all_to_all | solution.py:362
  47.0 0.0 copy-done
  47.0 0.0 copy-done.1
  47.0 0.0 copy-done.2
  47.0 0.0 copy-done.3
  47.0 2.8 %bed_first.1.before_ref = f32[8,128]{1,0:T(8,128)S(1)} custom-call(s32[3,1,128]{2,1,0:T(1,128)S(1)} %copy-done.2, s32[3,32768]{1,0:T(4,128)S(1)} %copy-done.3, f32[256,128]{1,0:T(8,128)S(1)} %bitcast.19, f32[256,128]{1,0:T(8,128)S(1)} %bitcast.21), custom_call_target="tpu_custom_call" | custom-call | flops 1000000000 | bytes 10000000 | tf_op jit(solution)/shard_map/bed_first/pallas_call | solution.py:443
  49.9 4.1 %bed_second.1 = (f32[8,128]{1,0:T(8,128)S(1)}, f32[256,128]{1,0:T(8,128)S(1)}, f32[256,128]{1,0:T(8,128)S(1)}) custom-call(s32[3,1,128]{2,1,0:T(1,128)S(1)} %copy-done.2, s32[3,32768]{1,0:T(4,128)S(1)} %copy-done.3, s32[768,128]{1,0:T(8,128)S(1)} %bitcast.17, f32[8,128]{1,0:T(8,128)S(1)} %bed_first.1.before_ref), custom_call_target="tpu_custom_call" | custom-call | flops 1000000000 | bytes 10000000 | tf_op jit(solution)/shard_map/bed_second/pallas_call | solution.py:464
  54.0 7.2 %all-to-all-done.1 = s32[128,1,768]{2,1,0:T(1,128)S(1)} async-done(((s32[128,1,768]{2,1,0:T(1,128)}), s32[128,1,768]{2,1,0:T(1,128)S(1)}, u32[]{:S(2)}, u32[]{:S(2)}) %all-to-all-start.1) | async-done | bytes 393248 | tf_op jit(solution)/shard_map/all_to_all | solution.py:362
  61.2 1.3 %bed_third.1 = (f32[4,128]{1,0:T(4,128)S(1)}, f32[4,128]{1,0:T(4,128)S(1)}) custom-call(f32[256,128]{1,0:T(8,128)S(1)} %get-tuple-element.34.row_ref, f32[256,128]{1,0:T(8,128)S(1)} %get-tuple-element.35.column_ref, s32[768,128]{1,0:T(8,128)S(1)} %bitcast.14, f32[8,128]{1,0:T(8,128)S(1)} %get-tuple-element.36.before_ref), custom_call_target="tpu_custom_call" | custom-call | tf_op jit(solution)/shard_map/bed_third/pallas_call | solution.py:477
  62.5 4.6 %collective-permute-start.2 = (f32[4,128]{1,0:T(4,128)S(1)}, f32[4,128]{1,0:T(4,128)S(1)}, u32[]{:S(2)}, u32[]{:S(2)}) collective-permute-start(f32[4,128]{1,0:T(4,128)S(1)} %get-tuple-element.38), channel_id=1, source_target_pairs={{0,128},{128,0},{1,129},{129,1},{2,130},{130,2},{3,131},{131,3},{4... | collective-permute-start | bytes 6152 | tf_op jit(solution)/shard_map/ppermute | solution.py:489
  67.0 1.1 %finish.1 = (f32[3,32768]{1,0:T(4,128)}, f32[256,128]{1,0:T(8,128)}) custom-call(s32[768,128]{1,0:T(8,128)S(1)} %bitcast.15, f32[128,8,128]{2,1,0:T(8,128)S(1)} %get-tuple-element.31.add_ref), custom_call_target="tpu_custom_call" | custom-call | flops 10000000 | bytes 1000000 | tf_op jit(solution)/shard_map/finish/pallas_call | solution.py:491
  68.1 0.0 collective-permute-done.2
  68.1 0.6 add.3
Async XLA Ops:
  0.6 5.1 %collective-permute-start = (bf16[3,4,2048]{2,1,0:T(4,128)(2,1)}, bf16[3,4,2048]{2,1,0:T(4,128)(2,1)S(1)}, u32[]{:S(2)}, u32[]{:S(2)}) collective-permute-start(bf16[3,4,2048]{2,1,0:T(4,128)(2,1)} %bitcast.22), channel_id=1, source_target_pairs={{0,128},{128,0},{1,129},{129,1},{2,130},{130,2},{3,131},{131,3},{4... | collective-permute-start | bytes 147464 | tf_op jit(solution)/shard_map/ppermute | solution.py:373
  4.0 1.7 %collective-permute-start.1 = (bf16[4,2048]{1,0:T(4,128)(2,1)}, bf16[4,2048]{1,0:T(4,128)(2,1)S(1)}, u32[]{:S(2)}, u32[]{:S(2)}) collective-permute-start(bf16[4,2048]{1,0:T(4,128)(2,1)} %bitcast.25), channel_id=1, source_target_pairs={{0,128},{128,0},{1,129},{129,1},{2,130},{130,2},{3,131},{131,3},{4... | collective-permute-start | bytes 49160 | tf_op jit(solution)/shard_map/ppermute | solution.py:374
  9.1 30.0 %all-to-all-start = ((s32[128,1,768]{2,1,0:T(1,128)}), s32[128,1,768]{2,1,0:T(1,128)S(1)}, u32[]{:S(2)}, u32[]{:S(2)}) async-start(s32[128,1,768]{2,1,0:T(1,128)} %bitcast.8), calls=%async_computation | async-start | bytes 786432 | tf_op jit(solution)/shard_map/all_to_all | solution.py:362
  30.5 16.5 %copy-start = (f32[32768]{0:T(1024)S(1)}, f32[32768]{0:T(1024)}, u32[]{:S(2)}) copy-start(f32[32768]{0:T(1024)} %param.11) | copy-start | bytes 393220
  30.5 16.5 %copy-start.1 = (f32[32768]{0:T(1024)S(1)}, f32[32768]{0:T(1024)}, u32[]{:S(2)}) copy-start(f32[32768]{0:T(1024)} %param.12) | copy-start | bytes 393220
  30.5 16.5 %copy-start.2 = (s32[3,1,128]{2,1,0:T(1,128)S(1)}, s32[3,1,128]{2,1,0:T(1,128)}, u32[]{:S(2)}) copy-start(s32[3,1,128]{2,1,0:T(1,128)} %tile_ref.5) | copy-start | bytes 4612
  30.6 16.5 %copy-start.3 = (s32[3,32768]{1,0:T(4,128)S(1)}, s32[3,32768]{1,0:T(4,128)}, u32[]{:S(2)}) copy-start(s32[3,32768]{1,0:T(4,128)} %bed_ref.3) | copy-start | bytes 1179652
  40.3 20.9 %all-to-all-start.1 = ((s32[128,1,768]{2,1,0:T(1,128)}), s32[128,1,768]{2,1,0:T(1,128)S(1)}, u32[]{:S(2)}, u32[]{:S(2)}) async-start(s32[128,1,768]{2,1,0:T(1,128)} %bitcast.10), calls=%async_computation.1 | async-start | bytes 786432 | tf_op jit(solution)/shard_map/all_to_all | solution.py:362
  62.5 5.6 %collective-permute-start.2 = (f32[4,128]{1,0:T(4,128)S(1)}, f32[4,128]{1,0:T(4,128)S(1)}, u32[]{:S(2)}, u32[]{:S(2)}) collective-permute-start(f32[4,128]{1,0:T(4,128)S(1)} %get-tuple-element.38), channel_id=1, source_target_pairs={{0,128},{128,0},{1,129},{129,1},{2,130},{130,2},{3,131},{131,3},{4... | collective-permute-start | bytes 6152 | tf_op jit(solution)/shard_map/ppermute | solution.py:489
